TPU v7x, 128 devices: a whole 4x4x4 slice. The times are simulated.
128 devices in a mesh: tm: 16 (over y, x), patch: 8 (over z, core).
Axes of the slice: x: 4, y: 4, z: 4, core: 2. Of those that a mesh axis runs over, the one named last changes fastest.
Arguments:
- snapshots: bfloat16 [128, 8192, 256], P('tm', 'patch'), may hold values from -6 to 6
- neighbours: int32 [8192, 5], P('patch'), may hold values from 0 to 8191, as said below
- owners: int32 [8192], P('patch'), may hold values from 0 to 2047, as said below
- w_mix1: bfloat16 [1280, 256], replicated, may hold values from -0.15625 to 0.15625
- w_mix2: bfloat16 [256, 256], replicated, may hold values from -0.375 to 0.375
- w_lift: bfloat16 [256, 512], replicated, may hold values from -0.375 to 0.375
- gain_attn: float32 [512], replicated, may hold values from 0.5 to 10
- w_qkv: bfloat16 [512, 1536], replicated, may hold values from -0.25 to 0.25
- w_out: bfloat16 [512, 512], replicated, may hold values from -0.25 to 0.25
- gain_ffn: float32 [512], replicated, may hold values from 0.1 to 1.9
- w_gate: bfloat16 [512, 2048], replicated, may hold values from -0.25 to 0.25
- w_up: bfloat16 [512, 2048], replicated, may hold values from -0.25 to 0.25
- w_down: bfloat16 [2048, 512], replicated, may hold values from -0.125 to 0.125
- w_dec: bfloat16 [512, 256], replicated, may hold values from -0.25 to 0.25
Outputs:
- decoded: bfloat16 [128, 8192, 256], P('tm', 'patch')
Inputs may be any that keep to these rules, and one draw needn't show every extreme that they name: neighbours[e, 0] is e; every entry lies within 64 of e in edge order and inside 0 to 8191; some entries lie exactly 64 away. owners[e] for an edge of patch p (edges 1024 * p to 1024 * (p + 1) - 1) is a coarse edge of that patch, 256 * p to 256 * (p + 1) - 1; every coarse edge is named by one or more fine edges.
All inputs are finite; a program needn't handle non-finite values.
Results may differ from a plain program's by a relative error of at most 0.04.
The roundings to bfloat16 on the way count: a program that leaves them out, or rounds other values in their place, can miss the bound.
Values may be sent and summed in bfloat16 or wider, within the bound.
No kernel may reach another device: no remote copies, remote signals or barrier semaphores. Data moves between devices by JAX's collectives and lax.ppermute only.
A program may use at most 192 MiB of HBM per device.

v0:
```python
import functools

import jax
import jax.numpy as jnp
from jax import lax
from jax.experimental import pallas as pl
from jax.experimental.pallas import tpu as pltpu
from jax.sharding import PartitionSpec as P

HEADS = 8
HALO = 64
TILE = 128
C = 256
DC = 512
FFN = 2048
S_DEV = 8
E_DEV = 1024
CC = 256
GROUPS = 16
HALVES = 2
HC = CC // GROUPS // HALVES
ROWS = HC * 128
eps_norm = 1e-05
bf16 = jnp.bfloat16
f32 = jnp.float32
VMEM_LIMIT = 48 * 1024 * 1024


def dot(a, b):
    return jnp.dot(a, b, preferred_element_type=f32)


def gelu(x):
    inner = 0.7978845608028654 * (x + 0.044715 * (x * x * x))
    return 0.5 * x * (1.0 + jnp.tanh(inner))


def pick_rows(ids_row, width=2 * TILE):
    across = jnp.broadcast_to(ids_row, (TILE, TILE)).astype(f32)
    down = across.T.astype(jnp.int32)
    lanes = lax.broadcasted_iota(jnp.int32, (TILE, TILE), 1)
    parts = [(down == lanes + TILE * i).astype(f32).astype(bf16) for i in range(width // TILE)]
    return jnp.concatenate(parts, axis=1)


def inner_kernel(nbr, x, w1, w2, out, pick, gath):
    first = lax.axis_index("patch") * E_DEV

    @pl.when(pl.program_id(0) == 0)
    def _():
        for j in range(1, 7):
            for k in range(1, 5):
                ids = nbr[k : k + 1, j * TILE : (j + 1) * TILE] - (first + j * TILE - HALO)
                pick[j - 1, (k - 1) * TILE : k * TILE, :] = pick_rows(ids)

    for j in range(1, 7):
        window = x[0, j * TILE - HALO : j * TILE + TILE + HALO, :]
        got = dot(pick[j - 1], window).astype(bf16)
        for k in range(1, 5):
            gath[(j - 1) * TILE : j * TILE, k * C : (k + 1) * C] = got[(k - 1) * TILE : k * TILE]
    centre = x[0, TILE : 7 * TILE, :]
    pre = dot(centre, w1[0:C, :]) + dot(gath[:, C:], w1[C:, :])
    act = gelu(pre).astype(bf16)
    out[0] = (centre.astype(f32) + dot(act, w2[...])).astype(bf16)


def inner(nbr_t, x, w1, w2):
    return pl.pallas_call(
        inner_kernel,
        grid=(S_DEV,),
        in_specs=[
            pl.BlockSpec((5, E_DEV), lambda s: (0, 0)),
            pl.BlockSpec((1, E_DEV, C), lambda s: (s, 0, 0)),
            pl.BlockSpec((5 * C, C), lambda s: (0, 0)),
            pl.BlockSpec((C, C), lambda s: (0, 0)),
        ],
        out_specs=pl.BlockSpec((1, 6 * TILE, C), lambda s: (s, 0, 0)),
        out_shape=jax.ShapeDtypeStruct((S_DEV, 6 * TILE, C), bf16),
        scratch_shapes=[
            pltpu.VMEM((6, 4 * TILE, 2 * TILE), bf16),
            pltpu.VMEM((6 * TILE, 5 * C), bf16),
        ],
        compiler_params=pltpu.CompilerParams(vmem_limit_bytes=VMEM_LIMIT),
        cost_estimate=pl.CostEstimate(flops=8 * 10**9, bytes_accessed=8 * 2**20, transcendentals=2**20),
        name="inner",
    )(nbr_t, x, w1, w2)


SB = 2


def edge_kernel(nbr, own, lo, hi, before, after, mid, w1, w2, edge, send_a, send_b, pick, gath, hot, rec, *sums):
    patch = lax.axis_index("patch")
    step = pl.program_id(0)

    @pl.when(step == 0)
    def _():
        for i, j in enumerate((0, 7)):
            for k in range(1, 5):
                ids = nbr[k : k + 1, j * TILE : (j + 1) * TILE] - (patch * E_DEV + j * TILE - HALO)
                pick[i, (k - 1) * TILE : k * TILE, :] = pick_rows(ids)
        slots = own[...] - patch * CC
        rows = lax.broadcasted_iota(jnp.int32, (CC, E_DEV), 0)
        onehot = (rows == slots).astype(f32)
        hot[...] = onehot.astype(bf16)
        counts = jnp.sum(onehot, axis=1, keepdims=True)
        rec[...] = jnp.broadcast_to(counts, (CC, TILE))

    for s in range(SB):
        low = jnp.concatenate([before[s]] + [lo[s, i] for i in range(3)], axis=0)
        high = jnp.concatenate([hi[s, i] for i in range(1, 4)] + [after[s]], axis=0)
        for i, window in enumerate((low, high)):
            got = dot(pick[i], window).astype(bf16)
            base = (2 * s + i) * TILE
            gath[base : base + TILE, 0:C] = window[HALO : HALO + TILE]
            for k in range(1, 5):
                gath[base : base + TILE, k * C : (k + 1) * C] = got[(k - 1) * TILE : k * TILE]
    act = gelu(dot(gath[...], w1[...])).astype(bf16)
    mixed = (gath[:, 0:C].astype(f32) + dot(act, w2[...])).astype(bf16)
    counts = rec[...]
    counts = jnp.concatenate([counts, counts], axis=1)
    for s in range(SB):
        both = mixed[2 * s * TILE : 2 * (s + 1) * TILE]
        edge[s] = both
        total = dot(hot[:, 0:TILE], both[0:TILE]) + dot(hot[:, 7 * TILE :], both[TILE:])
        total = total + dot(hot[:, TILE : 7 * TILE], mid[s])
        mean = total / counts
        for i in range(2):
            sums[i][pl.ds(step * SB + s, CC, stride=S_DEV), :] = mean[:, i * 128 : (i + 1) * 128]

    @pl.when(step == S_DEV // SB - 1)
    def _():
        block = HC * S_DEV
        for g in range(GROUPS):
            for i in range(2):
                cols = slice(i * 128, (i + 1) * 128)
                send_a[g, :, cols] = sums[i][(2 * g) * block : (2 * g + 1) * block, :].astype(bf16)
                send_b[g, :, cols] = sums[i][(2 * g + 1) * block : (2 * g + 2) * block, :].astype(bf16)


def edges(nbr_t, own, x4, before, after, mid, w1, w2):
    fixed2 = lambda s: (0, 0)
    send = jax.ShapeDtypeStruct((GROUPS, HC * S_DEV, C), bf16)
    return pl.pallas_call(
        edge_kernel,
        grid=(S_DEV // SB,),
        in_specs=[
            pl.BlockSpec((5, E_DEV), fixed2),
            pl.BlockSpec((1, E_DEV), fixed2),
            pl.BlockSpec((SB, 4, HALO, C), lambda s: (s, 0, 0, 0)),
            pl.BlockSpec((SB, 4, HALO, C), lambda s: (s, 3, 0, 0)),
            pl.BlockSpec((SB, HALO, C), lambda s: (s, 0, 0)),
            pl.BlockSpec((SB, HALO, C), lambda s: (s, 0, 0)),
            pl.BlockSpec((SB, 6 * TILE, C), lambda s: (s, 0, 0)),
            pl.BlockSpec((5 * C, C), fixed2),
            pl.BlockSpec((C, C), fixed2),
        ],
        out_specs=[
            pl.BlockSpec((SB, 2 * TILE, C), lambda s: (s, 0, 0)),
            pl.BlockSpec((GROUPS, HC * S_DEV, C), lambda s: (0, 0, 0)),
            pl.BlockSpec((GROUPS, HC * S_DEV, C), lambda s: (0, 0, 0)),
        ],
        out_shape=[jax.ShapeDtypeStruct((S_DEV, 2 * TILE, C), bf16), send, send],
        scratch_shapes=[
            pltpu.VMEM((2, 4 * TILE, 2 * TILE), bf16),
            pltpu.VMEM((SB * 2 * TILE, 5 * C), bf16),
            pltpu.VMEM((CC, E_DEV), bf16),
            pltpu.VMEM((CC, TILE), f32),
            pltpu.VMEM((CC * S_DEV, 128), f32),
            pltpu.VMEM((CC * S_DEV, 128), f32),
        ],
        compiler_params=pltpu.CompilerParams(vmem_limit_bytes=VMEM_LIMIT),
        cost_estimate=pl.CostEstimate(flops=4 * 10**9, bytes_accessed=8 * 2**20, transcendentals=2**19),
        name="edges",
    )(nbr_t, own, x4, x4, before, after, mid, w1, w2)


RB = 512
FB = 512


def rms(rows, gain):
    mean_sq = jnp.mean(rows * rows, axis=-1, keepdims=True)
    return (rows * lax.rsqrt(mean_sq + eps_norm) * gain).astype(bf16)


def layer_kernel(
    x, ga, gf, lift_h, qkv_h, out_h, gate_h, up_h, down_h, dec_h, y,
    lift, wqkv, wout, gate, up, down, dec, flat, qkv, lifted, att, normed, acc, sems,
):
    copies = [
        pltpu.make_async_copy(src, dst, sems.at[i])
        for i, (src, dst) in enumerate(
            (
                (lift_h, lift), (qkv_h, wqkv), (out_h, wout), (gate_h, gate),
                (up_h, up), (down_h, down), (dec_h, dec),
            )
        )
    ]
    for copy in copies:
        copy.start()
    for g in range(GROUPS):
        part = x[g].astype(f32)
        for c in range(HC):
            flat[c * 128 + g * S_DEV : c * 128 + (g + 1) * S_DEV, :] = part[c * S_DEV : (c + 1) * S_DEV]
    lane = lax.broadcasted_iota(jnp.int32, (128, 256), 1) // 64
    causal = lax.broadcasted_iota(jnp.int32, (512, 128), 1) <= (
        lax.broadcasted_iota(jnp.int32, (512, 128), 0) % 128
    )

    def block(b, _):
        r0 = b * RB
        if not isinstance(b, int):
            r0 = pl.multiple_of(r0, RB)

        rows = flat[pl.ds(r0, RB), :].astype(bf16)
        low = dot(rows, lift[...]).astype(bf16)
        lifted[...] = low
        normed[...] = rms(low.astype(f32), ga[...])
        qkv[...] = dot(normed[...], wqkv[...]).astype(bf16)
        for c in range(RB // 128):
            sl = slice(c * 128, (c + 1) * 128)
            for half in range(2):
                q = qkv[sl, half * 256 : half * 256 + 256].astype(f32) * 0.125
                k = qkv[sl, DC + half * 256 : DC + half * 256 + 256]
                v = qkv[sl, 2 * DC + half * 256 : 2 * DC + half * 256 + 256]
                stacked = jnp.concatenate(
                    [jnp.where(lane == h, q, 0.0).astype(bf16) for h in range(4)], axis=0
                )
                scores = lax.dot_general(
                    stacked, k, (((1,), (1,)), ((), ())), preferred_element_type=f32
                )
                scores = jnp.where(causal, scores, -jnp.inf)
                top = jnp.max(scores, axis=-1, keepdims=True)
                e = jnp.exp(scores - top)
                weights = (e / jnp.sum(e, axis=-1, keepdims=True)).astype(bf16)
                full = dot(weights, v)
                o = full[0:128]
                for h in range(1, 4):
                    o = jnp.where(lane == h, full[h * 128 : (h + 1) * 128], o)
                att[sl, half * 256 : half * 256 + 256] = o.astype(bf16)
        one = (lifted[...].astype(f32) + dot(att[...], wout[...])).astype(bf16).astype(f32)
        acc[...] = one
        normed[...] = rms(one, gf[...])
        for n in range(FFN // FB):
            cols = slice(n * FB, (n + 1) * FB)
            g = dot(normed[...], gate[:, cols])
            u = dot(normed[...], up[:, cols])
            hidden = (g * (1.0 / (1.0 + jnp.exp(-g))) * u).astype(bf16)
            acc[...] += dot(hidden, down[cols, :])
        flat[pl.ds(r0, RB), :] = dot(acc[...].astype(bf16), dec[...])
        return 0

    for copy in copies:
        copy.wait()
    lax.fori_loop(0, ROWS // RB, block, 0)
    for g in range(GROUPS):
        y[g] = jnp.concatenate(
            [flat[c * 128 + g * S_DEV : c * 128 + (g + 1) * S_DEV, :] for c in range(HC)], axis=0
        ).astype(bf16)


def layer(x, ga, gf, weights):
    vm = pl.BlockSpec(memory_space=pltpu.VMEM)
    hbm = pl.BlockSpec(memory_space=pl.ANY)
    return pl.pallas_call(
        layer_kernel,
        in_specs=[vm, vm, vm] + [hbm] * 7,
        out_specs=vm,
        out_shape=jax.ShapeDtypeStruct((GROUPS, HC * S_DEV, C), bf16),
        scratch_shapes=[pltpu.VMEM(w.shape, bf16) for w in weights]
        + [
            pltpu.VMEM((ROWS, C), f32),
            pltpu.VMEM((RB, 3 * DC), bf16),
            pltpu.VMEM((RB, DC), bf16),
            pltpu.VMEM((RB, DC), bf16),
            pltpu.VMEM((RB, DC), bf16),
            pltpu.VMEM((RB, DC), f32),
            pltpu.SemaphoreType.DMA((7,)),
        ],
        compiler_params=pltpu.CompilerParams(vmem_limit_bytes=VMEM_LIMIT),
        cost_estimate=pl.CostEstimate(flops=12 * 10**9, bytes_accessed=10 * 2**20, transcendentals=2**22),
        name="layer",
    )(x, ga, gf, *weights)


def spread_kernel(hot, mid, edge, back_a, back_b, out, *flat):
    @pl.when(pl.program_id(0) == 0)
    def _():
        for h in range(2):
            cols = slice(h * 128, (h + 1) * 128)
            flat[h][0:ROWS, :] = back_a[:, cols].astype(f32)
            flat[h][ROWS:, :] = back_b[:, cols].astype(f32)

    for i in range(SB):
        s = pl.program_id(0) * SB + i
        coarse = jnp.concatenate(
            [flat[h][pl.ds(s, CC, stride=S_DEV), :].astype(bf16) for h in range(2)], axis=1
        )
        out[i, 0:TILE, :] = (edge[i, 0:TILE].astype(f32) + dot(hot[0:TILE], coarse)).astype(bf16)
        out[i, TILE : 7 * TILE, :] = (
            mid[i].astype(f32) + dot(hot[TILE : 7 * TILE], coarse)
        ).astype(bf16)
        out[i, 7 * TILE :, :] = (
            edge[i, TILE:].astype(f32) + dot(hot[7 * TILE :], coarse)
        ).astype(bf16)


def spread(hot, mid, edge, back_a, back_b):
    return pl.pallas_call(
        spread_kernel,
        grid=(S_DEV // SB,),
        in_specs=[
            pl.BlockSpec((E_DEV, CC), lambda s: (0, 0)),
            pl.BlockSpec((SB, 6 * TILE, C), lambda s: (s, 0, 0)),
            pl.BlockSpec((SB, 2 * TILE, C), lambda s: (s, 0, 0)),
            pl.BlockSpec((ROWS, C), lambda s: (0, 0)),
            pl.BlockSpec((ROWS, C), lambda s: (0, 0)),
        ],
        out_specs=pl.BlockSpec((SB, E_DEV, C), lambda s: (s, 0, 0)),
        out_shape=jax.ShapeDtypeStruct((S_DEV, E_DEV, C), bf16),
        scratch_shapes=[pltpu.VMEM((2 * ROWS, 128), f32)] * 2,
        compiler_params=pltpu.CompilerParams(vmem_limit_bytes=VMEM_LIMIT),
        cost_estimate=pl.CostEstimate(flops=10**9, bytes_accessed=9 * 2**20, transcendentals=0),
        name="spread",
    )(hot, mid, edge, back_a, back_b)


def exchange(x):
    return lax.all_to_all(x, "tm", split_axis=0, concat_axis=0, tiled=True)


def per_device(
    snapshots, neighbours, owners, w_mix1, w_mix2, w_lift, gain_attn, w_qkv, w_out,
    gain_ffn, w_gate, w_up, w_down, w_dec,
):
    n_patch = lax.axis_size("patch")
    up = [(i, i + 1) for i in range(n_patch - 1)]
    down = [(j, i) for i, j in up]
    before = lax.ppermute(snapshots[:, E_DEV - HALO :], "patch", up)
    after = lax.ppermute(snapshots[:, :HALO], "patch", down)
    nbr_t = neighbours.T
    mid = inner(nbr_t, snapshots, w_mix1, w_mix2)
    x4 = snapshots.reshape(S_DEV, E_DEV // HALO, HALO, C)
    edge, send_a, send_b = edges(
        nbr_t, owners.reshape(1, E_DEV), x4, before, after, mid, w_mix1, w_mix2
    )
    weights = (w_lift, w_qkv, w_out, w_gate, w_up, w_down, w_dec)
    ga, gf = gain_attn.reshape(1, DC), gain_ffn.reshape(1, DC)
    series_a = exchange(send_a)
    series_b = exchange(send_b)
    done_a = layer(series_a, ga, gf, weights)
    back_a = exchange(done_a)
    done_b = layer(series_b, ga, gf, weights)
    back_b = exchange(done_b)
    slots = owners - lax.axis_index("patch") * CC
    group, rest = slots // (2 * HC), slots % (2 * HC)
    place = (rest // HC) * (CC // 2) + group * HC + rest % HC
    hot = (place[:, None] == jnp.arange(CC, dtype=jnp.int32)[None, :]).astype(bf16)
    return spread(
        hot, mid, edge, back_a.reshape(ROWS, C), back_b.reshape(ROWS, C)
    )


def solution(mesh):
    in_specs = (P("tm", "patch", None), P("patch", None), P("patch")) + (P(),) * 11
    return jax.shard_map(
        per_device, mesh=mesh, in_specs=in_specs, out_specs=P("tm", "patch", None), check_vma=False
    )
```

profile of v0, /device:TPU:32, one launch (start us, length us, event | category | flops | bytes accessed | tf_op | source)
XLA Modules:
  0.0 142.1 jit_solution(8634320200967577044)
XLA Ops:
  0.0 1.1 fusion.11
  1.1 1.9 %collective-permute-start.1 = (bf16[8,64,256]{2,1,0:T(8,128)(2,1)S(1)}, bf16[8,64,256]{2,1,0:T(8,128)(2,1)S(1)}, u32[]{:S(2)}, u32[]{:S(2)}) collective-permute-start(bf16[8,64,256]{2,1,0:T(8,128)(2,1)S(1)} %get-tuple-element.11), channel_id=1, source_target_pairs={{1,0},{2,1},{3,2},{4,3},{5,4},{6,5},{7,6},{9,8},{10,9},{11,10},{12... | collective-permute-start | bytes 786440 | tf_op jit(solution)/shard_map/ppermute | solution.py:341
  3.0 2.4 %collective-permute-start = (bf16[8,64,256]{2,1,0:T(8,128)(2,1)S(1)}, bf16[8,64,256]{2,1,0:T(8,128)(2,1)S(1)}, u32[]{:S(2)}, u32[]{:S(2)}) collective-permute-start(bf16[8,64,256]{2,1,0:T(8,128)(2,1)S(1)} %get-tuple-element.12), channel_id=1, source_target_pairs={{0,1},{1,2},{2,3},{3,4},{4,5},{5,6},{6,7},{8,9},{9,10},{10,11},{11... | collective-permute-start | bytes 786440 | tf_op jit(solution)/shard_map/ppermute | solution.py:340
  5.4 1.1 copy-done.12
  8.2 13.1 %inner.1.mid = bf16[8,768,256]{2,1,0:T(8,128)(2,1)S(1)} custom-call(s32[5,1024]{1,0:T(8,128)S(1)} %bitcast.8, bf16[8,1024,256]{2,1,0:T(8,128)(2,1)} %x.1, bf16[1280,256]{1,0:T(8,128)(2,1)S(1)} %copy-done.12, bf16[256,256]{1,0:T(8,128)(2,1)S(1)} %copy-done.19), custom_call_target="tpu_custom_call" | custom-call | flops 8000000000 | bytes 8388608 | tf_op jit(solution)/shard_map/inner/pallas_call | solution.py:68
  21.3 1.7 %copy-done = bf16[8,768,256]{2,1,0:T(8,128)(2,1)} copy-done((bf16[8,768,256]{2,1,0:T(8,128)(2,1)}, bf16[8,768,256]{2,1,0:T(8,128)(2,1)S(1)}, u32[]{:S(2)}) %copy-start) | copy-done | bytes 3145752
  23.0 11.1 %edges.1 = (bf16[8,256,256]{2,1,0:T(8,128)(2,1)S(1)}, bf16[16,64,256]{2,1,0:T(8,128)(2,1)S(1)}, bf16[16,64,256]{2,1,0:T(8,128)(2,1)}) custom-call(s32[5,1024]{1,0:T(8,128)S(1)} %bitcast.9, s32[1,1024]{1,0:T(1,128)S(1)} %bitcast.7, bf16[8,16,64,256]{3,2,1,0:T(8,128)(2,1)} %bitcast.14, bf16[8,16,64,256]{3,2,1,0:T(8,128)(2,1)} %bitcast.15, ...), custom_call_target="tpu_custom_call" | custom-call | flops 4000000000 | bytes 8388608 | tf_op jit(solution)/shard_map/edges/pallas_call | solution.py:144
  35.1 19.5 %all_to_all.20.x = bf16[16,64,256]{2,1,0:T(8,128)(2,1)S(1)} all-to-all(bf16[16,64,256]{2,1,0:T(8,128)(2,1)S(1)} %get-tuple-element.9), channel_id=1, replica_groups=mesh['tm'=16,'patch'=8] {'tm'}, dimensions={0} | all-to-all | bytes 1048576 | tf_op jit(solution)/shard_map/all_to_all | solution.py:330
  54.6 4.2 %all-to-all-start.2 = ((bf16[16,64,256]{2,1,0:T(8,128)(2,1)}), bf16[16,64,256]{2,1,0:T(8,128)(2,1)}, u32[]{:S(2)}, u32[]{:S(2)}) async-start(bf16[16,64,256]{2,1,0:T(8,128)(2,1)} %get-tuple-element.10), calls=%async_computation.2 | async-start | bytes 1048576 | tf_op jit(solution)/shard_map/all_to_all | solution.py:330
  58.9 1.6 %copy-done.8 = bf16[512,2048]{1,0:T(8,128)(2,1)S(1)} copy-done((bf16[512,2048]{1,0:T(8,128)(2,1)S(1)}, bf16[512,2048]{1,0:T(8,128)(2,1)}, u32[]{:S(2)}) %copy-start.8) | copy-done | bytes 2097176
  60.5 1.4 copy-done.10
  61.9 1.0 copy-done.14
  63.9 18.9 %layer.2 = bf16[16,64,256]{2,1,0:T(8,128)(2,1)S(1)} custom-call(bf16[16,64,256]{2,1,0:T(8,128)(2,1)S(1)} %all_to_all.20.x, f32[1,512]{1,0:T(1,128)S(1)} %bitcast.10, f32[1,512]{1,0:T(1,128)S(1)} %bitcast.12, bf16[256,512]{1,0:T(8,128)(2,1)S(1)} %copy-done.16, bf16[512,1536]{1,0:T(8,128)(2,1)S(1)} %copy-done.10, bf16[512,512]{1,0:T(8,128)(2,1)S(1)} %copy-done.14, ...), custom_call_target="tpu_custom_call" | custom-call | flops 12000000000 | bytes 10485760 | tf_op jit(solution)/shard_map/layer/pallas_call | solution.py:266
  83.6 7.1 %all-to-all-start.1 = ((bf16[16,64,256]{2,1,0:T(8,128)(2,1)}), bf16[16,64,256]{2,1,0:T(8,128)(2,1)}, u32[]{:S(2)}, u32[]{:S(2)}) async-start(bf16[16,64,256]{2,1,0:T(8,128)(2,1)} %copy-done.6), calls=%async_computation.1 | async-start | bytes 1048576 | tf_op jit(solution)/shard_map/all_to_all | solution.py:330
  90.8 1.6 %copy-done.9 = bf16[512,2048]{1,0:T(8,128)(2,1)S(1)} copy-done((bf16[512,2048]{1,0:T(8,128)(2,1)S(1)}, bf16[512,2048]{1,0:T(8,128)(2,1)}, u32[]{:S(2)}) %copy-start.9) | copy-done | bytes 2097176
  92.4 1.4 copy-done.11
  93.8 1.0 copy-done.15
  95.8 20.1 %layer.3 = bf16[16,64,256]{2,1,0:T(8,128)(2,1)S(1)} custom-call(bf16[16,64,256]{2,1,0:T(8,128)(2,1)} %all-to-all-done.2.x, f32[1,512]{1,0:T(1,128)S(1)} %bitcast.11, f32[1,512]{1,0:T(1,128)S(1)} %bitcast.13, bf16[256,512]{1,0:T(8,128)(2,1)S(1)} %copy-done.16, bf16[512,1536]{1,0:T(8,128)(2,1)S(1)} %copy-done.11, bf16[512,512]{1,0:T(8,128)(2,1)S(1)} %copy-done.15, ...), custom_call_target="tpu_custom_call" | custom-call | flops 12000000000 | bytes 10485760 | tf_op jit(solution)/shard_map/layer/pallas_call | solution.py:266
  116.7 7.2 %all-to-all-start.3 = ((bf16[16,64,256]{2,1,0:T(8,128)(2,1)}), bf16[16,64,256]{2,1,0:T(8,128)(2,1)}, u32[]{:S(2)}, u32[]{:S(2)}) async-start(bf16[16,64,256]{2,1,0:T(8,128)(2,1)} %copy-done.5), calls=%async_computation.3 | async-start | bytes 1048576 | tf_op jit(solution)/shard_map/all_to_all | solution.py:330
  123.9 1.0 fusion.hot
  124.9 10.0 %all-to-all-done.3 = bf16[16,64,256]{2,1,0:T(8,128)(2,1)} async-done(((bf16[16,64,256]{2,1,0:T(8,128)(2,1)}), bf16[16,64,256]{2,1,0:T(8,128)(2,1)}, u32[]{:S(2)}, u32[]{:S(2)}) %all-to-all-start.3) | async-done | bytes 524320 | tf_op jit(solution)/shard_map/all_to_all | solution.py:330
  135.0 1.0 copy-done.2
  136.0 1.2 copy-done.4
  137.2 4.8 %spread.1 = bf16[8,1024,256]{2,1,0:T(8,128)(2,1)} custom-call(bf16[1024,256]{1,0:T(8,128)(2,1)S(1)} %copy-done.2, bf16[8,768,256]{2,1,0:T(8,128)(2,1)S(1)} %copy-done.1, bf16[8,256,256]{2,1,0:T(8,128)(2,1)S(1)} %copy-done.4, bf16[1024,256]{1,0:T(8,128)(2,1)} %bitcast.5.back_a, bf16[1024,256]{1,0:T(8,128)(2,1)} %bitcast.6.back_b), custom_call_target="tpu_custom_call" | custom-call | flops 1000000000 | bytes 9437184 | tf_op jit(solution)/shard_map/spread/pallas_call | solution.py:310
  (45 shorter events, 6.2 us)
Async XLA Ops:
  1.1 21.9 %collective-permute-start.1 = (bf16[8,64,256]{2,1,0:T(8,128)(2,1)S(1)}, bf16[8,64,256]{2,1,0:T(8,128)(2,1)S(1)}, u32[]{:S(2)}, u32[]{:S(2)}) collective-permute-start(bf16[8,64,256]{2,1,0:T(8,128)(2,1)S(1)} %get-tuple-element.11), channel_id=1, source_target_pairs={{1,0},{2,1},{3,2},{4,3},{5,4},{6,5},{7,6},{9,8},{10,9},{11,10},{12... | collective-permute-start | bytes 786440 | tf_op jit(solution)/shard_map/ppermute | solution.py:341
  3.0 20.0 %collective-permute-start = (bf16[8,64,256]{2,1,0:T(8,128)(2,1)S(1)}, bf16[8,64,256]{2,1,0:T(8,128)(2,1)S(1)}, u32[]{:S(2)}, u32[]{:S(2)}) collective-permute-start(bf16[8,64,256]{2,1,0:T(8,128)(2,1)S(1)} %get-tuple-element.12), channel_id=1, source_target_pairs={{0,1},{1,2},{2,3},{3,4},{4,5},{5,6},{6,7},{8,9},{9,10},{10,11},{11... | collective-permute-start | bytes 786440 | tf_op jit(solution)/shard_map/ppermute | solution.py:340
  5.4 1.1 copy-start.12
  8.2 14.8 %copy-start.7 = (s32[1024]{0:T(1024)S(1)}, s32[1024]{0:T(1024)}, u32[]{:S(2)}) copy-start(s32[1024]{0:T(1024)} %param.16) | copy-start | bytes 12292
  8.2 14.8 %copy-start.13 = (bf16[1280,256]{1,0:T(8,128)(2,1)S(1)}, bf16[1280,256]{1,0:T(8,128)(2,1)}, u32[]{:S(2)}) copy-start(bf16[1280,256]{1,0:T(8,128)(2,1)} %w1.3) | copy-start | bytes 1966084
  8.2 14.8 %copy-start.20 = (bf16[256,256]{1,0:T(8,128)(2,1)S(1)}, bf16[256,256]{1,0:T(8,128)(2,1)}, u32[]{:S(2)}) copy-start(bf16[256,256]{1,0:T(8,128)(2,1)} %w2.3) | copy-start | bytes 393220
  8.2 14.8 %copy-start.22 = (s32[1024,5]{0,1:T(8,128)S(1)}, s32[1024,5]{0,1:T(8,128)}, u32[]{:S(2)}) copy-start(s32[1024,5]{0,1:T(8,128)} %param.15) | copy-start | bytes 61444
  21.3 1.7 %copy-start = (bf16[8,768,256]{2,1,0:T(8,128)(2,1)}, bf16[8,768,256]{2,1,0:T(8,128)(2,1)S(1)}, u32[]{:S(2)}) copy-start(bf16[8,768,256]{2,1,0:T(8,128)(2,1)S(1)} %inner.1.mid) | copy-start | bytes 9437188
  23.0 35.9 %copy-start.16 = (bf16[256,512]{1,0:T(8,128)(2,1)S(1)}, bf16[256,512]{1,0:T(8,128)(2,1)}, u32[]{:S(2)}) copy-start(bf16[256,512]{1,0:T(8,128)(2,1)} %lift_h.3) | copy-start | bytes 786436
  23.0 35.9 %copy-start.23 = (f32[512]{0:T(512)S(1)}, f32[512]{0:T(512)}, u32[]{:S(2)}) copy-start(f32[512]{0:T(512)} %param.20) | copy-start | bytes 6148
  23.0 35.9 %copy-start.24 = (f32[512]{0:T(512)S(1)}, f32[512]{0:T(512)}, u32[]{:S(2)}) copy-start(f32[512]{0:T(512)} %param.23) | copy-start | bytes 6148
  34.2 1.0 copy-start.3
  54.6 29.0 %all-to-all-start.2 = ((bf16[16,64,256]{2,1,0:T(8,128)(2,1)}), bf16[16,64,256]{2,1,0:T(8,128)(2,1)}, u32[]{:S(2)}, u32[]{:S(2)}) async-start(bf16[16,64,256]{2,1,0:T(8,128)(2,1)} %get-tuple-element.10), calls=%async_computation.2 | async-start | bytes 1048576 | tf_op jit(solution)/shard_map/all_to_all | solution.py:330
  58.9 1.6 %copy-start.8 = (bf16[512,2048]{1,0:T(8,128)(2,1)S(1)}, bf16[512,2048]{1,0:T(8,128)(2,1)}, u32[]{:S(2)}) copy-start(bf16[512,2048]{1,0:T(8,128)(2,1)} %gate_h.3) | copy-start | bytes 6291460
  60.5 1.4 copy-start.10
  61.9 1.0 copy-start.14
  83.6 33.1 %all-to-all-start.1 = ((bf16[16,64,256]{2,1,0:T(8,128)(2,1)}), bf16[16,64,256]{2,1,0:T(8,128)(2,1)}, u32[]{:S(2)}, u32[]{:S(2)}) async-start(bf16[16,64,256]{2,1,0:T(8,128)(2,1)} %copy-done.6), calls=%async_computation.1 | async-start | bytes 1048576 | tf_op jit(solution)/shard_map/all_to_all | solution.py:330
  90.8 1.6 %copy-start.9 = (bf16[512,2048]{1,0:T(8,128)(2,1)S(1)}, bf16[512,2048]{1,0:T(8,128)(2,1)}, u32[]{:S(2)}) copy-start(bf16[512,2048]{1,0:T(8,128)(2,1)} %gate_h.3) | copy-start | bytes 6291460
  92.4 1.4 copy-start.11
  93.8 1.0 copy-start.15
  95.8 39.2 %copy-start.1 = (bf16[8,768,256]{2,1,0:T(8,128)(2,1)S(1)}, bf16[8,768,256]{2,1,0:T(8,128)(2,1)}, u32[]{:S(2)}) copy-start(bf16[8,768,256]{2,1,0:T(8,128)(2,1)} %copy-done) | copy-start | bytes 9437188
  116.7 18.3 %all-to-all-start.3 = ((bf16[16,64,256]{2,1,0:T(8,128)(2,1)}), bf16[16,64,256]{2,1,0:T(8,128)(2,1)}, u32[]{:S(2)}, u32[]{:S(2)}) async-start(bf16[16,64,256]{2,1,0:T(8,128)(2,1)} %copy-done.5), calls=%async_computation.3 | async-start | bytes 1048576 | tf_op jit(solution)/shard_map/all_to_all | solution.py:330
  135.0 1.0 copy-start.2
  136.0 1.2 copy-start.4
  (6 other events, 5.2 us)
where the time goes:
time: 144 us; the launch traced here: 142 us
  Pallas kernels  68.1 us (47%)
  starting transfers between devices  22.9 us (16%)
  local copies, waits for them, and re-layouts  20.3 us (14%)
  blocking collectives  19.5 us (14%)
  waiting for transfers between devices  10 us (7%)
    pallas_call x2, Pallas kernels, layer(): pl.pallas_call(layer_kernel, in_specs=[vm, vm, vm] + [hbm] * 7, out_specs...  39 us
    all_to_all x1, blocking collectives, exchange(): return lax.all_to_all(x, 'tm', split_axis=0, concat_axis=0, tiled=True)  19.5 us
    unnamed x50, local copies, waits for them, and re-layouts  19.2 us
    all_to_all x3, starting transfers between devices, exchange(): return lax.all_to_all(x, 'tm', split_axis=0, concat_axis=0, tiled=True)  18.6 us
    pallas_call x1, Pallas kernels, inner(): pl.pallas_call(inner_kernel, grid=(S_DEV,), in_specs=[pl.BlockSpec((5, E_...  13.1 us
    pallas_call x1, Pallas kernels, edges(): pl.pallas_call(edge_kernel, grid=(S_DEV // SB,), in_specs=[pl.BlockSpec((...  11.1 us
    all_to_all x3, waiting for transfers between devices, exchange(): return lax.all_to_all(x, 'tm', split_axis=0, concat_axis=0, tiled=True)  10 us
    pallas_call x1, Pallas kernels, spread(): pl.pallas_call(spread_kernel, grid=(S_DEV // SB,), in_specs=[pl.BlockSpec...  4.85 us
  transfers between devices with their start and end apart: 5, of which 1 were waited for; matrix products, arithmetic and copies ran while one was open for 1% of the time, Pallas kernels for 37%

commit v1 on v0

v1 whole, which is shorter than its diff:
```python
import functools

import jax
import jax.numpy as jnp
from jax import lax
from jax.experimental import pallas as pl
from jax.experimental.pallas import tpu as pltpu
from jax.sharding import PartitionSpec as P

HEADS = 8
HALO = 64
TILE = 128
C = 256
DC = 512
FFN = 2048
S_DEV = 8
E_DEV = 1024
CC = 256
GROUPS = 16
HC = CC // GROUPS
ROWS = HC * 128
eps_norm = 1e-05
bf16 = jnp.bfloat16
f32 = jnp.float32
vm = pl.BlockSpec(memory_space=pltpu.VMEM)
hbm = pl.BlockSpec(memory_space=pltpu.HBM)


def dot(a, b):
    return jnp.dot(a, b, preferred_element_type=f32)


def gelu(x):
    inner = 0.7978845608028654 * (x + 0.044715 * (x * x * x))
    return 0.5 * x * (1.0 + jnp.tanh(inner))


def pick_rows(ids_row, width=2 * TILE):
    across = jnp.broadcast_to(ids_row, (TILE, TILE)).astype(f32)
    down = across.T.astype(jnp.int32)
    lanes = lax.broadcasted_iota(jnp.int32, (TILE, TILE), 1)
    parts = [(down == lanes + TILE * i).astype(f32).astype(bf16) for i in range(width // TILE)]
    return jnp.concatenate(parts, axis=1)


def mix_kernel(
    nbr_h, own_h, x_h, w1_h, w2_h, before, after, mixed_h, send,
    nbr, own, x, w1, w2, mixed, sems, out_sems, pick, gath, hot, counts, *sums,
):
    small = [
        pltpu.make_async_copy(src, dst, sems.at[S_DEV + i])
        for i, (src, dst) in enumerate(((nbr_h, nbr), (own_h, own), (w1_h, w1), (w2_h, w2)))
    ]

    def load(s):
        return pltpu.make_async_copy(x_h.at[s], x.at[s], sems.at[s])

    def save(s):
        return pltpu.make_async_copy(mixed.at[s], mixed_h.at[s], out_sems.at[s])

    for copy in small:
        copy.start()
    for s in range(S_DEV):
        load(s).start()
    small[0].wait()
    small[1].wait()
    patch = lax.axis_index("patch")
    for j in range(8):
        for k in range(1, 5):
            ids = nbr[k : k + 1, j * TILE : (j + 1) * TILE] - (patch * E_DEV + j * TILE - HALO)
            pick[j, (k - 1) * TILE : k * TILE, :] = pick_rows(ids)
    slots = own[...] - patch * CC
    rows = lax.broadcasted_iota(jnp.int32, (CC, E_DEV), 0)
    onehot = (rows == slots).astype(f32)
    hot[...] = onehot.astype(bf16)
    counts[...] = jnp.broadcast_to(jnp.sum(onehot, axis=1, keepdims=True), (CC, TILE))

    small[2].wait()
    small[3].wait()

    def gather(s, base):
        for j in range(8):
            if j == 0:
                window = jnp.concatenate([before[s], x[s, 0 : TILE + HALO]], axis=0)
            elif j == 7:
                window = jnp.concatenate([x[s, E_DEV - TILE - HALO :], after[s]], axis=0)
            else:
                window = x[s, j * TILE - HALO : j * TILE + TILE + HALO]
            got = dot(pick[j], window).astype(bf16)
            to = slice(base + j * TILE, base + (j + 1) * TILE)
            for k in range(4):
                gath[to, k * C : (k + 1) * C] = got[k * TILE : (k + 1) * TILE]

    def snapshots(b, _):
        for i in range(SB):
            load(b * SB + i).wait()
        for i in range(SB):
            gather(b * SB + i, i * E_DEV)
        centre = x[pl.ds(b * SB, SB)].reshape(SB * E_DEV, C)
        pre = dot(centre, w1[0:C, :]) + dot(gath[...], w1[C:, :])
        act = gelu(pre).astype(bf16)
        both = (centre.astype(f32) + dot(act, w2[...])).astype(bf16)
        mixed[pl.ds(b * SB, SB)] = both.reshape(SB, E_DEV, C)
        for i in range(SB):
            save(b * SB + i).start()
        for i in range(SB):
            total = dot(hot[...], both[i * E_DEV : (i + 1) * E_DEV])
            for h in range(2):
                mean = total[:, h * TILE : (h + 1) * TILE] / counts[...]
                sums[h][pl.ds(b * SB + i, CC, stride=S_DEV), :] = mean
        return 0

    lax.fori_loop(0, S_DEV // SB, snapshots, 0)
    for g in range(GROUPS):
        for i in range(2):
            send[g, :, i * TILE : (i + 1) * TILE] = sums[i][
                g * HC * S_DEV : (g + 1) * HC * S_DEV, :
            ].astype(bf16)
    for s in range(S_DEV):
        save(s).wait()


SB = 2


def mix(nbr_t, own, x, before, after, w1, w2):
    return pl.pallas_call(
        mix_kernel,
        in_specs=[hbm] * 5 + [vm] * 2,
        out_specs=[hbm, vm],
        out_shape=[
            pltpu.HBM((S_DEV, E_DEV, C), bf16),
            jax.ShapeDtypeStruct((GROUPS, HC * S_DEV, C), bf16),
        ],
        scratch_shapes=[
            pltpu.VMEM((5, E_DEV), jnp.int32),
            pltpu.VMEM((1, E_DEV), jnp.int32),
            pltpu.VMEM((S_DEV, E_DEV, C), bf16),
            pltpu.VMEM((5 * C, C), bf16),
            pltpu.VMEM((C, C), bf16),
            pltpu.VMEM((S_DEV, E_DEV, C), bf16),
            pltpu.SemaphoreType.DMA((S_DEV + 4,)),
            pltpu.SemaphoreType.DMA((S_DEV,)),
            pltpu.VMEM((8, 4 * TILE, 2 * TILE), bf16),
            pltpu.VMEM((SB * E_DEV, 4 * C), bf16),
            pltpu.VMEM((CC, E_DEV), bf16),
            pltpu.VMEM((CC, TILE), f32),
            pltpu.VMEM((CC * S_DEV, TILE), f32),
            pltpu.VMEM((CC * S_DEV, TILE), f32),
        ],
        compiler_params=pltpu.CompilerParams(vmem_limit_bytes=36 * 2**20),
        cost_estimate=pl.CostEstimate(flops=12 * 10**9, bytes_accessed=2**20, transcendentals=2**21),
        name="mix",
    )(in_hbm(nbr_t), in_hbm(own), in_hbm(x), in_hbm(w1), in_hbm(w2), before, after)


RB = 1024
FB = 256


def rms(rows, gain):
    mean_sq = jnp.mean(rows * rows, axis=-1, keepdims=True)
    return (rows * lax.rsqrt(mean_sq + eps_norm) * gain).astype(bf16)


def layer_kernel(
    x, ga, gf, lift, wqkv, wout, gate, up, down, dec, y,
    flat, qkv, lifted, att, normed, acc, hidden,
):
    for g in range(GROUPS):
        part = x[g].astype(f32)
        for c in range(HC):
            flat[c * 128 + g * S_DEV : c * 128 + (g + 1) * S_DEV, :] = part[c * S_DEV : (c + 1) * S_DEV]
    lane = lax.broadcasted_iota(jnp.int32, (128, 256), 1) // 64
    causal = lax.broadcasted_iota(jnp.int32, (512, 128), 1) <= (
        lax.broadcasted_iota(jnp.int32, (512, 128), 0) % 128
    )

    def block(b, _):
        r0 = b * RB
        if not isinstance(b, int):
            r0 = pl.multiple_of(r0, RB)

        rows = flat[pl.ds(r0, RB), :].astype(bf16)
        low = dot(rows, lift[...]).astype(bf16)
        lifted[...] = low
        normed[...] = rms(low.astype(f32), ga[...])
        qkv[...] = dot(normed[...], wqkv[...]).astype(bf16)
        for c in range(RB // 128):
            sl = slice(c * 128, (c + 1) * 128)
            for half in range(2):
                q = qkv[sl, half * 256 : half * 256 + 256].astype(f32) * 0.125
                k = qkv[sl, DC + half * 256 : DC + half * 256 + 256]
                v = qkv[sl, 2 * DC + half * 256 : 2 * DC + half * 256 + 256]
                stacked = jnp.concatenate(
                    [jnp.where(lane == h, q, 0.0).astype(bf16) for h in range(4)], axis=0
                )
                scores = lax.dot_general(
                    stacked, k, (((1,), (1,)), ((), ())), preferred_element_type=f32
                )
                scores = jnp.where(causal, scores, -jnp.inf)
                top = jnp.max(scores, axis=-1, keepdims=True)
                e = jnp.exp(scores - top)
                share = 1.0 / jnp.sum(e, axis=-1, keepdims=True)
                full = dot(e.astype(bf16), v) * share
                o = full[0:128]
                for h in range(1, 4):
                    o = jnp.where(lane == h, full[h * 128 : (h + 1) * 128], o)
                att[sl, half * 256 : half * 256 + 256] = o.astype(bf16)
        one = (lifted[...].astype(f32) + dot(att[...], wout[...])).astype(bf16).astype(f32)
        acc[...] = one
        normed[...] = rms(one, gf[...])
        for n in range(FFN // FB):
            cols = slice(n * FB, (n + 1) * FB)
            g = dot(normed[...], gate[:, cols])
            u = dot(normed[...], up[:, cols])
            hidden[:, cols] = (g * (1.0 / (1.0 + jnp.exp(-g))) * u).astype(bf16)
        two = (acc[...] + dot(hidden[...], down[...])).astype(bf16)
        flat[pl.ds(r0, RB), :] = dot(two, dec[...])
        return 0

    lax.fori_loop(0, ROWS // RB, block, 0)
    for g in range(GROUPS):
        y[g] = jnp.concatenate(
            [flat[c * 128 + g * S_DEV : c * 128 + (g + 1) * S_DEV, :] for c in range(HC)], axis=0
        ).astype(bf16)


def layer(x, ga, gf, weights):
    return pl.pallas_call(
        layer_kernel,
        in_specs=[vm] * 10,
        out_specs=vm,
        out_shape=jax.ShapeDtypeStruct((GROUPS, HC * S_DEV, C), bf16),
        scratch_shapes=[
            pltpu.VMEM((ROWS, C), f32),
            pltpu.VMEM((RB, 3 * DC), bf16),
            pltpu.VMEM((RB, DC), bf16),
            pltpu.VMEM((RB, DC), bf16),
            pltpu.VMEM((RB, DC), bf16),
            pltpu.VMEM((RB, DC), f32),
            pltpu.VMEM((RB, FFN), bf16),
        ],
        compiler_params=pltpu.CompilerParams(vmem_limit_bytes=32 * 2**20),
        cost_estimate=pl.CostEstimate(flops=24 * 10**9, bytes_accessed=2**20, transcendentals=2**22),
        name="layer",
    )(x, ga, gf, *weights)


def spread_kernel(mixed_h, hot, back, out_h, stage, in_sems, out_sems, *flat):
    def load(s):
        return pltpu.make_async_copy(mixed_h.at[s], stage.at[s], in_sems.at[s])

    def save(s):
        return pltpu.make_async_copy(stage.at[s], out_h.at[s], out_sems.at[s])

    for s in range(S_DEV):
        load(s).start()
    for h in range(2):
        flat[h][...] = back[:, h * TILE : (h + 1) * TILE].astype(f32)
    for s in range(S_DEV):
        coarse = jnp.concatenate(
            [flat[h][pl.ds(s, CC, stride=S_DEV), :].astype(bf16) for h in range(2)], axis=1
        )
        load(s).wait()
        stage[s] = (stage[s].astype(f32) + dot(hot[...], coarse)).astype(bf16)
        save(s).start()
    for s in range(S_DEV):
        save(s).wait()


def spread(mixed, hot, back):
    return pl.pallas_call(
        spread_kernel,
        in_specs=[hbm, vm, vm],
        out_specs=hbm,
        out_shape=jax.ShapeDtypeStruct((S_DEV, E_DEV, C), bf16),
        scratch_shapes=[
            pltpu.VMEM((S_DEV, E_DEV, C), bf16),
            pltpu.SemaphoreType.DMA((S_DEV,)),
            pltpu.SemaphoreType.DMA((S_DEV,)),
            pltpu.VMEM((ROWS, TILE), f32),
            pltpu.VMEM((ROWS, TILE), f32),
        ],
        compiler_params=pltpu.CompilerParams(vmem_limit_bytes=24 * 2**20),
        cost_estimate=pl.CostEstimate(flops=10**9, bytes_accessed=8 * 2**20, transcendentals=0),
        name="spread",
    )(in_hbm(mixed), hot, back)


def in_hbm(array):
    return pltpu.with_memory_space_constraint(array, pltpu.HBM)


def exchange(x):
    return lax.all_to_all(x, "tm", split_axis=0, concat_axis=0, tiled=True)


def per_device(
    snapshots, neighbours, owners, w_mix1, w_mix2, w_lift, gain_attn, w_qkv, w_out,
    gain_ffn, w_gate, w_up, w_down, w_dec,
):
    n_patch = lax.axis_size("patch")
    up = [(i, i + 1) for i in range(n_patch - 1)]
    down = [(j, i) for i, j in up]
    before = lax.ppermute(snapshots[:, E_DEV - HALO :], "patch", up)
    after = lax.ppermute(snapshots[:, :HALO], "patch", down)
    nbr_t = neighbours.T
    mixed, send = mix(
        nbr_t, owners.reshape(1, E_DEV), snapshots, before, after, w_mix1, w_mix2
    )
    weights = (w_lift, w_qkv, w_out, w_gate, w_up, w_down, w_dec)
    ga, gf = gain_attn.reshape(1, DC), gain_ffn.reshape(1, DC)
    back = exchange(layer(exchange(send), ga, gf, weights))
    slots = owners - lax.axis_index("patch") * CC
    hot = (slots[:, None] == jnp.arange(CC, dtype=jnp.int32)[None, :]).astype(bf16)
    return spread(mixed, hot, back.reshape(ROWS, C))


def solution(mesh):
    in_specs = (P("tm", "patch", None), P("patch", None), P("patch")) + (P(),) * 11
    return jax.shard_map(
        per_device, mesh=mesh, in_specs=in_specs, out_specs=P("tm", "patch", None), check_vma=False
    )
```

time: 144 us -> 107 us (0.74); the launches traced: 142 us -> 107 us
  local copies, waits for them, and re-layouts: 20.3 us -> 1.12 us
  Pallas kernels: 68.1 us -> 52.3 us
  starting transfers between devices: 22.9 us -> 8.2 us
  waiting for transfers between devices: 10 us -> 21.1 us
  blocking collectives: 19.5 us -> 23.7 us
    unnamed x50 -> x20, local copies, waits for them, and re-layouts: 19.2 us -> 0.05 us
    pallas_call x5 -> x3, Pallas kernels: 68.1 us -> 52.3 us  [the longest x1 27.4 us: layer(): pl.pallas_call(layer_kernel, in_specs=[vm] * 10, out_specs=vm, out_shape=...]
    all_to_all x3 -> x1, starting transfers between devices: 18.6 us -> 3.88 us  [exchange(): return lax.all_to_all(x, 'tm', split_axis=0, concat_axis=0, tiled=True)]
    all_to_all x3 -> x1, waiting for transfers between devices: 10 us -> 15.8 us  [exchange(): return lax.all_to_all(x, 'tm', split_axis=0, concat_axis=0, tiled=True)]
    all_to_all x1, blocking collectives: 19.5 us -> 23.7 us  [exchange(): return lax.all_to_all(x, 'tm', split_axis=0, concat_axis=0, tiled=True)]
    ppermute x1, waiting for transfers between devices: 0.01 us -> 3.82 us  [per_device(): before = lax.ppermute(snapshots[:, E_DEV - HALO:], 'patch', up)]
    ppermute x1, waiting for transfers between devices: 0.01 us -> 1.45 us  [per_device(): after = lax.ppermute(snapshots[:, :HALO], 'patch', down)]
  transfers between devices with their start and end apart: 5 -> 3, of which waited for: 1 -> 3; matrix products, arithmetic and copies ran while one was open for 1% -> 0% of each run, Pallas kernels for 37% -> 0%
where the time goes in v1:
time: 107 us
  Pallas kernels  52.3 us (49%)
  blocking collectives  23.7 us (22%)
  waiting for transfers between devices  21.1 us (20%)
  starting transfers between devices  8.2 us (8%)
  local copies, waits for them, and re-layouts  1.12 us (1%)
    pallas_call x1, Pallas kernels, layer(): pl.pallas_call(layer_kernel, in_specs=[vm] * 10, out_specs=vm, out_shape=...  27.4 us
    all_to_all x1, blocking collectives, exchange(): return lax.all_to_all(x, 'tm', split_axis=0, concat_axis=0, tiled=True)  23.7 us
    pallas_call x1, Pallas kernels, mix(): pl.pallas_call(mix_kernel, in_specs=[hbm] * 5 + [vm] * 2, out_specs=[hbm,...  19.3 us
    all_to_all x1, waiting for transfers between devices, exchange(): return lax.all_to_all(x, 'tm', split_axis=0, concat_axis=0, tiled=True)  15.8 us
    pallas_call x1, Pallas kernels, spread(): pl.pallas_call(spread_kernel, in_specs=[hbm, vm, vm], out_specs=hbm, out_...  5.64 us
    all_to_all x1, starting transfers between devices, exchange(): return lax.all_to_all(x, 'tm', split_axis=0, concat_axis=0, tiled=True)  3.88 us
    ppermute x1, waiting for transfers between devices, per_device(): before = lax.ppermute(snapshots[:, E_DEV - HALO:], 'patch', up)  3.82 us
    ppermute x1, starting transfers between devices, per_device(): before = lax.ppermute(snapshots[:, E_DEV - HALO:], 'patch', up)  2.41 us
  transfers between devices with their start and end apart: 3, of which 3 were waited for; matrix products, arithmetic and copies ran while one was open for 0% of the time, Pallas kernels for 0%

profile of v1, /device:TPU:32, one launch (start us, length us, event | category | flops | bytes accessed | tf_op | source)
XLA Modules:
  0.0 107.0 jit_solution(3904722268524995091)
XLA Ops:
  0.0 1.1 fusion.1
  1.1 1.9 %collective-permute-start.1 = (bf16[8,64,256]{2,1,0:T(8,128)(2,1)S(1)}, bf16[8,64,256]{2,1,0:T(8,128)(2,1)S(1)}, u32[]{:S(2)}, u32[]{:S(2)}) collective-permute-start(bf16[8,64,256]{2,1,0:T(8,128)(2,1)S(1)} %get-tuple-element.9), channel_id=1, source_target_pairs={{1,0},{2,1},{3,2},{4,3},{5,4},{6,5},{7,6},{9,8},{10,9},{11,10},{12... | collective-permute-start | bytes 786440 | tf_op jit(solution)/shard_map/ppermute | solution.py:307
  3.0 2.4 %collective-permute-start = (bf16[8,64,256]{2,1,0:T(8,128)(2,1)S(1)}, bf16[8,64,256]{2,1,0:T(8,128)(2,1)S(1)}, u32[]{:S(2)}, u32[]{:S(2)}) collective-permute-start(bf16[8,64,256]{2,1,0:T(8,128)(2,1)S(1)} %get-tuple-element.10), channel_id=1, source_target_pairs={{0,1},{1,2},{2,3},{3,4},{4,5},{5,6},{6,7},{8,9},{9,10},{10,11},{11... | collective-permute-start | bytes 786440 | tf_op jit(solution)/shard_map/ppermute | solution.py:306
  5.4 1.5 %collective-permute-done.1.after = bf16[8,64,256]{2,1,0:T(8,128)(2,1)S(1)} collective-permute-done((bf16[8,64,256]{2,1,0:T(8,128)(2,1)S(1)}, bf16[8,64,256]{2,1,0:T(8,128)(2,1)S(1)}, u32[]{:S(2)}, u32[]{:S(2)}) %collective-permute-start.1) | collective-permute-done | bytes 262176 | tf_op jit(solution)/shard_map/ppermute | solution.py:307
  6.9 3.8 %collective-permute-done.before = bf16[8,64,256]{2,1,0:T(8,128)(2,1)S(1)} collective-permute-done((bf16[8,64,256]{2,1,0:T(8,128)(2,1)S(1)}, bf16[8,64,256]{2,1,0:T(8,128)(2,1)S(1)}, u32[]{:S(2)}, u32[]{:S(2)}) %collective-permute-start) | collective-permute-done | bytes 262176 | tf_op jit(solution)/shard_map/ppermute | solution.py:306
  10.7 0.0 copy-start.4
  10.7 0.0 copy-start.5
  10.7 0.0 copy-start.6
  10.7 0.0 copy-start.7
  10.8 0.0 copy-start.8
  10.8 19.3 %mix.1 = (bf16[8,1024,256]{2,1,0:T(8,128)(2,1)}, bf16[16,128,256]{2,1,0:T(8,128)(2,1)S(1)}) custom-call(s32[5,1024]{1,0:T(8,128)} %bitcast.9, s32[1,1024]{1,0:T(1,128)} %bitcast.8, bf16[8,1024,256]{2,1,0:T(8,128)(2,1)} %x_h.1, bf16[1280,256]{1,0:T(8,128)(2,1)} %w1_h.1, bf16[256,256]{1,0:T(8,128)(2,1)} %w2_h.1, ...), custom_call_target="tpu_custom_call" | custom-call | flops 12000000000 | bytes 1048576 | tf_op jit(solution)/shard_map/mix/pallas_call | solution.py:127
  30.1 23.7 %all_to_all.10.x = bf16[16,128,256]{2,1,0:T(8,128)(2,1)S(1)} all-to-all(bf16[16,128,256]{2,1,0:T(8,128)(2,1)S(1)} %get-tuple-element.8), channel_id=1, replica_groups=mesh['tm'=16,'patch'=8] {'tm'}, dimensions={0} | all-to-all | bytes 2097152 | tf_op jit(solution)/shard_map/all_to_all | solution.py:296
  53.8 0.0 copy-done
  53.8 0.0 copy-done.1
  53.8 0.0 copy-done.2
  53.8 0.0 copy-done.3
  53.8 0.0 copy-done.4
  53.8 0.0 copy-done.5
  53.9 0.0 copy-start.9
  53.9 27.4 %layer.1 = bf16[16,128,256]{2,1,0:T(8,128)(2,1)} custom-call(bf16[16,128,256]{2,1,0:T(8,128)(2,1)S(1)} %all_to_all.10.x, f32[1,512]{1,0:T(1,128)S(1)} %bitcast.6, f32[1,512]{1,0:T(1,128)S(1)} %bitcast.7, bf16[256,512]{1,0:T(8,128)(2,1)S(1)} %copy-done.5, bf16[512,1536]{1,0:T(8,128)(2,1)S(1)} %copy-done.3, bf16[512,512]{1,0:T(8,128)(2,1)S(1)} %copy-done.4, ...), custom_call_target="tpu_custom_call" | custom-call | flops 24000000000 | bytes 1048576 | tf_op jit(solution)/shard_map/layer/pallas_call | solution.py:230
  81.3 3.9 %all-to-all-start.1 = ((bf16[16,128,256]{2,1,0:T(8,128)(2,1)}), bf16[16,128,256]{2,1,0:T(8,128)(2,1)S(1)}, u32[]{:S(2)}, u32[]{:S(2)}) async-start(bf16[16,128,256]{2,1,0:T(8,128)(2,1)} %layer.1), calls=%async_computation.1 | async-start | bytes 2097152 | tf_op jit(solution)/shard_map/all_to_all | solution.py:296
  85.2 0.2 fusion.hot
  85.4 15.8 %all-to-all-done.1 = bf16[16,128,256]{2,1,0:T(8,128)(2,1)S(1)} async-done(((bf16[16,128,256]{2,1,0:T(8,128)(2,1)}), bf16[16,128,256]{2,1,0:T(8,128)(2,1)S(1)}, u32[]{:S(2)}, u32[]{:S(2)}) %all-to-all-start.1) | async-done | bytes 1048608 | tf_op jit(solution)/shard_map/all_to_all | solution.py:296
  101.2 5.6 %spread.1 = bf16[8,1024,256]{2,1,0:T(8,128)(2,1)} custom-call(bf16[8,1024,256]{2,1,0:T(8,128)(2,1)} %get-tuple-element.7.mixed_h, bf16[1024,256]{1,0:T(8,128)(2,1)S(1)} %fusion.hot, bf16[2048,256]{1,0:T(8,128)(2,1)S(1)} %bitcast.5), custom_call_target="tpu_custom_call" | custom-call | flops 1000000000 | bytes 8388608 | tf_op jit(solution)/shard_map/spread/pallas_call | solution.py:273
  (9 shorter events, 0.0 us)
Async XLA Ops:
  1.1 5.8 %collective-permute-start.1 = (bf16[8,64,256]{2,1,0:T(8,128)(2,1)S(1)}, bf16[8,64,256]{2,1,0:T(8,128)(2,1)S(1)}, u32[]{:S(2)}, u32[]{:S(2)}) collective-permute-start(bf16[8,64,256]{2,1,0:T(8,128)(2,1)S(1)} %get-tuple-element.9), channel_id=1, source_target_pairs={{1,0},{2,1},{3,2},{4,3},{5,4},{6,5},{7,6},{9,8},{10,9},{11,10},{12... | collective-permute-start | bytes 786440 | tf_op jit(solution)/shard_map/ppermute | solution.py:307
  3.0 7.7 %collective-permute-start = (bf16[8,64,256]{2,1,0:T(8,128)(2,1)S(1)}, bf16[8,64,256]{2,1,0:T(8,128)(2,1)S(1)}, u32[]{:S(2)}, u32[]{:S(2)}) collective-permute-start(bf16[8,64,256]{2,1,0:T(8,128)(2,1)S(1)} %get-tuple-element.10), channel_id=1, source_target_pairs={{0,1},{1,2},{2,3},{3,4},{4,5},{5,6},{6,7},{8,9},{9,10},{10,11},{11... | collective-permute-start | bytes 786440 | tf_op jit(solution)/shard_map/ppermute | solution.py:306
  10.7 43.1 %copy-start = (bf16[512,2048]{1,0:T(8,128)(2,1)S(1)}, bf16[512,2048]{1,0:T(8,128)(2,1)}, u32[]{:S(2)}) copy-start(bf16[512,2048]{1,0:T(8,128)(2,1)} %gate.1) | copy-start | bytes 6291460
  10.7 43.1 %copy-start.1 = (bf16[512,2048]{1,0:T(8,128)(2,1)S(1)}, bf16[512,2048]{1,0:T(8,128)(2,1)}, u32[]{:S(2)}) copy-start(bf16[512,2048]{1,0:T(8,128)(2,1)} %up.1) | copy-start | bytes 6291460
  10.7 43.1 %copy-start.2 = (bf16[2048,512]{1,0:T(8,128)(2,1)S(1)}, bf16[2048,512]{1,0:T(8,128)(2,1)}, u32[]{:S(2)}) copy-start(bf16[2048,512]{1,0:T(8,128)(2,1)} %down.1) | copy-start | bytes 6291460
  10.7 43.1 %copy-start.3 = (bf16[512,1536]{1,0:T(8,128)(2,1)S(1)}, bf16[512,1536]{1,0:T(8,128)(2,1)}, u32[]{:S(2)}) copy-start(bf16[512,1536]{1,0:T(8,128)(2,1)} %wqkv.1) | copy-start | bytes 4718596
  10.7 43.1 %copy-start.4 = (bf16[512,512]{1,0:T(8,128)(2,1)S(1)}, bf16[512,512]{1,0:T(8,128)(2,1)}, u32[]{:S(2)}) copy-start(bf16[512,512]{1,0:T(8,128)(2,1)} %wout.1) | copy-start | bytes 1572868
  10.7 43.1 %copy-start.5 = (bf16[256,512]{1,0:T(8,128)(2,1)S(1)}, bf16[256,512]{1,0:T(8,128)(2,1)}, u32[]{:S(2)}) copy-start(bf16[256,512]{1,0:T(8,128)(2,1)} %lift.1) | copy-start | bytes 786436
  10.7 43.1 %copy-start.6 = (bf16[512,256]{1,0:T(8,128)(2,1)S(1)}, bf16[512,256]{1,0:T(8,128)(2,1)}, u32[]{:S(2)}) copy-start(bf16[512,256]{1,0:T(8,128)(2,1)} %dec.1) | copy-start | bytes 786436
  10.7 43.1 %copy-start.7 = (f32[512]{0:T(512)S(1)}, f32[512]{0:T(512)}, u32[]{:S(2)}) copy-start(f32[512]{0:T(512)} %param.20) | copy-start | bytes 6148
  10.8 43.1 %copy-start.8 = (f32[512]{0:T(512)S(1)}, f32[512]{0:T(512)}, u32[]{:S(2)}) copy-start(f32[512]{0:T(512)} %param.23) | copy-start | bytes 6148
  53.9 31.3 %copy-start.9 = (s32[1024]{0:T(1024)S(1)}, s32[1024]{0:T(1024)}, u32[]{:S(2)}) copy-start(s32[1024]{0:T(1024)} %param.16) | copy-start | bytes 12292
  81.3 19.9 %all-to-all-start.1 = ((bf16[16,128,256]{2,1,0:T(8,128)(2,1)}), bf16[16,128,256]{2,1,0:T(8,128)(2,1)S(1)}, u32[]{:S(2)}, u32[]{:S(2)}) async-start(bf16[16,128,256]{2,1,0:T(8,128)(2,1)} %layer.1), calls=%async_computation.1 | async-start | bytes 2097152 | tf_op jit(solution)/shard_map/all_to_all | solution.py:296

commit v2 on v1

--- a/solution.py
+++ b/solution.py
@@ -44,8 +44,8 @@
 
 
 def mix_kernel(
-    nbr_h, own_h, x_h, w1_h, w2_h, before, after, mixed_h, send,
-    nbr, own, x, w1, w2, mixed, sems, out_sems, pick, gath, hot, counts, *sums,
+    nbr_h, own_h, x_h, w1_h, w2_h, before, after, mixed, send, unpool,
+    nbr, own, x, w1, w2, sems, pick, gath, hot, share, *sums,
 ):
     small = [
         pltpu.make_async_copy(src, dst, sems.at[S_DEV + i])
@@ -54,9 +54,6 @@
 
     def load(s):
         return pltpu.make_async_copy(x_h.at[s], x.at[s], sems.at[s])
-
-    def save(s):
-        return pltpu.make_async_copy(mixed.at[s], mixed_h.at[s], out_sems.at[s])
 
     for copy in small:
         copy.start()
@@ -70,10 +67,12 @@
             ids = nbr[k : k + 1, j * TILE : (j + 1) * TILE] - (patch * E_DEV + j * TILE - HALO)
             pick[j, (k - 1) * TILE : k * TILE, :] = pick_rows(ids)
     slots = own[...] - patch * CC
+    for j in range(8):
+        unpool[j * TILE : (j + 1) * TILE, :] = pick_rows(slots[:, j * TILE : (j + 1) * TILE])
     rows = lax.broadcasted_iota(jnp.int32, (CC, E_DEV), 0)
     onehot = (rows == slots).astype(f32)
     hot[...] = onehot.astype(bf16)
-    counts[...] = jnp.broadcast_to(jnp.sum(onehot, axis=1, keepdims=True), (CC, TILE))
+    share[...] = jnp.broadcast_to(1.0 / jnp.sum(onehot, axis=1, keepdims=True), (CC, TILE))
 
     small[2].wait()
     small[3].wait()
@@ -102,11 +101,9 @@
         both = (centre.astype(f32) + dot(act, w2[...])).astype(bf16)
         mixed[pl.ds(b * SB, SB)] = both.reshape(SB, E_DEV, C)
         for i in range(SB):
-            save(b * SB + i).start()
-        for i in range(SB):
             total = dot(hot[...], both[i * E_DEV : (i + 1) * E_DEV])
             for h in range(2):
-                mean = total[:, h * TILE : (h + 1) * TILE] / counts[...]
+                mean = total[:, h * TILE : (h + 1) * TILE] * share[...]
                 sums[h][pl.ds(b * SB + i, CC, stride=S_DEV), :] = mean
         return 0
 
@@ -116,8 +113,6 @@
             send[g, :, i * TILE : (i + 1) * TILE] = sums[i][
                 g * HC * S_DEV : (g + 1) * HC * S_DEV, :
             ].astype(bf16)
-    for s in range(S_DEV):
-        save(s).wait()
 
 
 SB = 2
@@ -127,10 +122,11 @@
     return pl.pallas_call(
         mix_kernel,
         in_specs=[hbm] * 5 + [vm] * 2,
-        out_specs=[hbm, vm],
+        out_specs=[vm] * 3,
         out_shape=[
-            pltpu.HBM((S_DEV, E_DEV, C), bf16),
+            jax.ShapeDtypeStruct((S_DEV, E_DEV, C), bf16),
             jax.ShapeDtypeStruct((GROUPS, HC * S_DEV, C), bf16),
+            jax.ShapeDtypeStruct((E_DEV, CC), bf16),
         ],
         scratch_shapes=[
             pltpu.VMEM((5, E_DEV), jnp.int32),
@@ -138,9 +134,7 @@
             pltpu.VMEM((S_DEV, E_DEV, C), bf16),
             pltpu.VMEM((5 * C, C), bf16),
             pltpu.VMEM((C, C), bf16),
-            pltpu.VMEM((S_DEV, E_DEV, C), bf16),
             pltpu.SemaphoreType.DMA((S_DEV + 4,)),
-            pltpu.SemaphoreType.DMA((S_DEV,)),
             pltpu.VMEM((8, 4 * TILE, 2 * TILE), bf16),
             pltpu.VMEM((SB * E_DEV, 4 * C), bf16),
             pltpu.VMEM((CC, E_DEV), bf16),
@@ -148,7 +142,7 @@
             pltpu.VMEM((CC * S_DEV, TILE), f32),
             pltpu.VMEM((CC * S_DEV, TILE), f32),
         ],
-        compiler_params=pltpu.CompilerParams(vmem_limit_bytes=36 * 2**20),
+        compiler_params=pltpu.CompilerParams(vmem_limit_bytes=32 * 2**20),
         cost_estimate=pl.CostEstimate(flops=12 * 10**9, bytes_accessed=2**20, transcendentals=2**21),
         name="mix",
     )(in_hbm(nbr_t), in_hbm(own), in_hbm(x), in_hbm(w1), in_hbm(w2), before, after)
@@ -247,23 +241,17 @@
     )(x, ga, gf, *weights)
 
 
-def spread_kernel(mixed_h, hot, back, out_h, stage, in_sems, out_sems, *flat):
-    def load(s):
-        return pltpu.make_async_copy(mixed_h.at[s], stage.at[s], in_sems.at[s])
-
+def spread_kernel(mixed, hot, back, out_h, stage, out_sems, *flat):
     def save(s):
         return pltpu.make_async_copy(stage.at[s], out_h.at[s], out_sems.at[s])
 
-    for s in range(S_DEV):
-        load(s).start()
     for h in range(2):
         flat[h][...] = back[:, h * TILE : (h + 1) * TILE].astype(f32)
     for s in range(S_DEV):
         coarse = jnp.concatenate(
             [flat[h][pl.ds(s, CC, stride=S_DEV), :].astype(bf16) for h in range(2)], axis=1
         )
-        load(s).wait()
-        stage[s] = (stage[s].astype(f32) + dot(hot[...], coarse)).astype(bf16)
+        stage[s] = (mixed[s].astype(f32) + dot(hot[...], coarse)).astype(bf16)
         save(s).start()
     for s in range(S_DEV):
         save(s).wait()
@@ -272,12 +260,11 @@
 def spread(mixed, hot, back):
     return pl.pallas_call(
         spread_kernel,
-        in_specs=[hbm, vm, vm],
+        in_specs=[vm, vm, vm],
         out_specs=hbm,
         out_shape=jax.ShapeDtypeStruct((S_DEV, E_DEV, C), bf16),
         scratch_shapes=[
             pltpu.VMEM((S_DEV, E_DEV, C), bf16),
-            pltpu.SemaphoreType.DMA((S_DEV,)),
             pltpu.SemaphoreType.DMA((S_DEV,)),
             pltpu.VMEM((ROWS, TILE), f32),
             pltpu.VMEM((ROWS, TILE), f32),
@@ -285,7 +272,7 @@
         compiler_params=pltpu.CompilerParams(vmem_limit_bytes=24 * 2**20),
         cost_estimate=pl.CostEstimate(flops=10**9, bytes_accessed=8 * 2**20, transcendentals=0),
         name="spread",
-    )(in_hbm(mixed), hot, back)
+    )(mixed, hot, back)
 
 
 def in_hbm(array):
@@ -306,14 +293,12 @@
     before = lax.ppermute(snapshots[:, E_DEV - HALO :], "patch", up)
     after = lax.ppermute(snapshots[:, :HALO], "patch", down)
     nbr_t = neighbours.T
-    mixed, send = mix(
+    mixed, send, hot = mix(
         nbr_t, owners.reshape(1, E_DEV), snapshots, before, after, w_mix1, w_mix2
     )
     weights = (w_lift, w_qkv, w_out, w_gate, w_up, w_down, w_dec)
     ga, gf = gain_attn.reshape(1, DC), gain_ffn.reshape(1, DC)
     back = exchange(layer(exchange(send), ga, gf, weights))
-    slots = owners - lax.axis_index("patch") * CC
-    hot = (slots[:, None] == jnp.arange(CC, dtype=jnp.int32)[None, :]).astype(bf16)
     return spread(mixed, hot, back.reshape(ROWS, C))
 
 

time: 107 us -> 102 us (0.953)
  blocking collectives: 23.7 us -> 42.9 us
  waiting for transfers between devices: 21.1 us -> 5.28 us
  Pallas kernels: 52.3 us -> 48.1 us
  starting transfers between devices: 8.2 us -> 4.33 us
    all_to_all x1 -> x2, blocking collectives: 23.7 us -> 42.9 us  [exchange(): return lax.all_to_all(x, 'tm', split_axis=0, concat_axis=0, tiled=True)]
    all_to_all x1 -> x0, waiting for transfers between devices: 15.8 us -> none  [exchange(): return lax.all_to_all(x, 'tm', split_axis=0, concat_axis=0, tiled=True)]
    all_to_all x1 -> x0, starting transfers between devices: 3.88 us -> none  [exchange(): return lax.all_to_all(x, 'tm', split_axis=0, concat_axis=0, tiled=True)]
    pallas_call x2, Pallas kernels: 25 us -> 21.7 us  [the longest x1 19 us: mix(): pl.pallas_call(mix_kernel, in_specs=[hbm] * 5 + [vm] * 2, out_specs=[vm]...]
  transfers between devices with their start and end apart: 3 -> 2, of which waited for: 3 -> 2; matrix products, arithmetic and copies ran while one was open for 0% -> 0% of each run, Pallas kernels for 0% -> 0%
where the time goes in v2:
time: 102 us
  Pallas kernels  48.1 us (47%)
  blocking collectives  42.9 us (42%)
  waiting for transfers between devices  5.28 us (5%)
  starting transfers between devices  4.33 us (4%)
  local copies, waits for them, and re-layouts  1.11 us (1%)
    all_to_all x2, blocking collectives, exchange(): return lax.all_to_all(x, 'tm', split_axis=0, concat_axis=0, tiled=True)  42.9 us
    pallas_call x1, Pallas kernels, layer(): pl.pallas_call(layer_kernel, in_specs=[vm] * 10, out_specs=vm, out_shape=...  26.4 us
    pallas_call x1, Pallas kernels, mix(): pl.pallas_call(mix_kernel, in_specs=[hbm] * 5 + [vm] * 2, out_specs=[vm]...  19 us
    ppermute x1, waiting for transfers between devices, per_device(): before = lax.ppermute(snapshots[:, E_DEV - HALO:], 'patch', up)  3.82 us
    pallas_call x1, Pallas kernels, spread(): pl.pallas_call(spread_kernel, in_specs=[vm, vm, vm], out_specs=hbm, out_s...  2.7 us
    ppermute x1, starting transfers between devices, per_device(): before = lax.ppermute(snapshots[:, E_DEV - HALO:], 'patch', up)  2.41 us
  transfers between devices with their start and end apart: 2, of which 2 were waited for; matrix products, arithmetic and copies ran while one was open for 0% of the time, Pallas kernels for 0%

profile of v2, /device:TPU:32, one launch (start us, length us, event | category | flops | bytes accessed | tf_op | source)
XLA Modules:
  0.0 102.0 jit_solution(14856336300222163417)
XLA Ops:
  0.0 1.1 %fusion = (bf16[8,64,256]{2,1,0:T(8,128)(2,1)S(1)}, bf16[8,64,256]{2,1,0:T(8,128)(2,1)S(1)}) fusion(bf16[8,1024,256]{2,1,0:T(8,128)(2,1)} %x_h.1), kind=kLoop, calls=%fused_computation | loop fusion | bytes 1048576 | tf_op jit(solution)/shard_map/slice | solution.py:294
  1.1 1.9 %collective-permute-start.1 = (bf16[8,64,256]{2,1,0:T(8,128)(2,1)S(1)}, bf16[8,64,256]{2,1,0:T(8,128)(2,1)S(1)}, u32[]{:S(2)}, u32[]{:S(2)}) collective-permute-start(bf16[8,64,256]{2,1,0:T(8,128)(2,1)S(1)} %get-tuple-element.11), channel_id=1, source_target_pairs={{1,0},{2,1},{3,2},{4,3},{5,4},{6,5},{7,6},{9,8},{10,9},{11,10},{12... | collective-permute-start | bytes 786440 | tf_op jit(solution)/shard_map/ppermute | solution.py:294
  3.0 2.4 %collective-permute-start = (bf16[8,64,256]{2,1,0:T(8,128)(2,1)S(1)}, bf16[8,64,256]{2,1,0:T(8,128)(2,1)S(1)}, u32[]{:S(2)}, u32[]{:S(2)}) collective-permute-start(bf16[8,64,256]{2,1,0:T(8,128)(2,1)S(1)} %get-tuple-element.12), channel_id=1, source_target_pairs={{0,1},{1,2},{2,3},{3,4},{4,5},{5,6},{6,7},{8,9},{9,10},{10,11},{11... | collective-permute-start | bytes 786440 | tf_op jit(solution)/shard_map/ppermute | solution.py:293
  5.4 1.5 %collective-permute-done.1.after = bf16[8,64,256]{2,1,0:T(8,128)(2,1)S(1)} collective-permute-done((bf16[8,64,256]{2,1,0:T(8,128)(2,1)S(1)}, bf16[8,64,256]{2,1,0:T(8,128)(2,1)S(1)}, u32[]{:S(2)}, u32[]{:S(2)}) %collective-permute-start.1) | collective-permute-done | bytes 262176 | tf_op jit(solution)/shard_map/ppermute | solution.py:294
  6.9 3.8 %collective-permute-done.before = bf16[8,64,256]{2,1,0:T(8,128)(2,1)S(1)} collective-permute-done((bf16[8,64,256]{2,1,0:T(8,128)(2,1)S(1)}, bf16[8,64,256]{2,1,0:T(8,128)(2,1)S(1)}, u32[]{:S(2)}, u32[]{:S(2)}) %collective-permute-start) | collective-permute-done | bytes 262176 | tf_op jit(solution)/shard_map/ppermute | solution.py:293
  10.7 0.0 copy-start.4
  10.7 0.0 copy-start.5
  10.7 0.0 copy-start.6
  10.7 0.0 copy-start.7
  10.7 0.0 copy-start.8
  10.8 19.0 %mix.1 = (bf16[8,1024,256]{2,1,0:T(8,128)(2,1)S(1)}, bf16[16,128,256]{2,1,0:T(8,128)(2,1)S(1)}, bf16[1024,256]{1,0:T(8,128)(2,1)S(1)}) custom-call(s32[5,1024]{1,0:T(8,128)} %bitcast.8, s32[1,1024]{1,0:T(1,128)} %bitcast.9, bf16[8,1024,256]{2,1,0:T(8,128)(2,1)} %x_h.1, bf16[1280,256]{1,0:T(8,128)(2,1)} %w1_h.1, bf16[256,256]{1,0:T(8,128)(2,1)} %w2_h.1, ...), custom_call_target="tpu_custom_call" | custom-call | flops 12000000000 | bytes 1048576 | tf_op jit(solution)/shard_map/mix/pallas_call | solution.py:122
  29.7 23.7 %all_to_all.10.x = bf16[16,128,256]{2,1,0:T(8,128)(2,1)S(1)} all-to-all(bf16[16,128,256]{2,1,0:T(8,128)(2,1)S(1)} %get-tuple-element.10), channel_id=1, replica_groups=mesh['tm'=16,'patch'=8] {'tm'}, dimensions={0} | all-to-all | bytes 2097152 | tf_op jit(solution)/shard_map/all_to_all | solution.py:283
  53.4 0.0 copy-done
  53.4 0.0 copy-done.1
  53.4 0.0 copy-done.2
  53.4 0.0 copy-done.3
  53.4 0.0 copy-done.4
  53.5 0.0 copy-done.5
  53.5 0.0 copy-done.6
  53.5 0.0 copy-done.7
  53.5 0.0 copy-done.8
  53.5 26.4 %layer.1 = bf16[16,128,256]{2,1,0:T(8,128)(2,1)S(1)} custom-call(bf16[16,128,256]{2,1,0:T(8,128)(2,1)S(1)} %all_to_all.10.x, f32[1,512]{1,0:T(1,128)S(1)} %bitcast.6, f32[1,512]{1,0:T(1,128)S(1)} %bitcast.7, bf16[256,512]{1,0:T(8,128)(2,1)S(1)} %copy-done.5, bf16[512,1536]{1,0:T(8,128)(2,1)S(1)} %copy-done.3, bf16[512,512]{1,0:T(8,128)(2,1)S(1)} %copy-done.4, ...), custom_call_target="tpu_custom_call" | custom-call | flops 24000000000 | bytes 1048576 | tf_op jit(solution)/shard_map/layer/pallas_call | solution.py:224
  79.9 19.2 %all_to_all.11 = bf16[16,128,256]{2,1,0:T(8,128)(2,1)S(1)} all-to-all(bf16[16,128,256]{2,1,0:T(8,128)(2,1)S(1)} %layer.1), channel_id=1, replica_groups=mesh['tm'=16,'patch'=8] {'tm'}, dimensions={0} | all-to-all | bytes 2097152 | tf_op jit(solution)/shard_map/all_to_all | solution.py:283
  99.1 2.7 %spread.1 = bf16[8,1024,256]{2,1,0:T(8,128)(2,1)} custom-call(bf16[8,1024,256]{2,1,0:T(8,128)(2,1)S(1)} %get-tuple-element.8.mixed, bf16[1024,256]{1,0:T(8,128)(2,1)S(1)} %get-tuple-element.9.hot, bf16[2048,256]{1,0:T(8,128)(2,1)S(1)} %bitcast.5), custom_call_target="tpu_custom_call" | custom-call | flops 1000000000 | bytes 8388608 | tf_op jit(solution)/shard_map/spread/pallas_call | solution.py:261
  (4 shorter events, 0.0 us)
Async XLA Ops:
  1.1 5.8 %collective-permute-start.1 = (bf16[8,64,256]{2,1,0:T(8,128)(2,1)S(1)}, bf16[8,64,256]{2,1,0:T(8,128)(2,1)S(1)}, u32[]{:S(2)}, u32[]{:S(2)}) collective-permute-start(bf16[8,64,256]{2,1,0:T(8,128)(2,1)S(1)} %get-tuple-element.11), channel_id=1, source_target_pairs={{1,0},{2,1},{3,2},{4,3},{5,4},{6,5},{7,6},{9,8},{10,9},{11,10},{12... | collective-permute-start | bytes 786440 | tf_op jit(solution)/shard_map/ppermute | solution.py:294
  3.0 7.7 %collective-permute-start = (bf16[8,64,256]{2,1,0:T(8,128)(2,1)S(1)}, bf16[8,64,256]{2,1,0:T(8,128)(2,1)S(1)}, u32[]{:S(2)}, u32[]{:S(2)}) collective-permute-start(bf16[8,64,256]{2,1,0:T(8,128)(2,1)S(1)} %get-tuple-element.12), channel_id=1, source_target_pairs={{0,1},{1,2},{2,3},{3,4},{4,5},{5,6},{6,7},{8,9},{9,10},{10,11},{11... | collective-permute-start | bytes 786440 | tf_op jit(solution)/shard_map/ppermute | solution.py:293
  10.7 42.7 %copy-start = (bf16[512,2048]{1,0:T(8,128)(2,1)S(1)}, bf16[512,2048]{1,0:T(8,128)(2,1)}, u32[]{:S(2)}) copy-start(bf16[512,2048]{1,0:T(8,128)(2,1)} %gate.1) | copy-start | bytes 6291460
  10.7 42.7 %copy-start.1 = (bf16[512,2048]{1,0:T(8,128)(2,1)S(1)}, bf16[512,2048]{1,0:T(8,128)(2,1)}, u32[]{:S(2)}) copy-start(bf16[512,2048]{1,0:T(8,128)(2,1)} %up.1) | copy-start | bytes 6291460
  10.7 42.7 %copy-start.2 = (bf16[2048,512]{1,0:T(8,128)(2,1)S(1)}, bf16[2048,512]{1,0:T(8,128)(2,1)}, u32[]{:S(2)}) copy-start(bf16[2048,512]{1,0:T(8,128)(2,1)} %down.1) | copy-start | bytes 6291460
  10.7 42.7 %copy-start.3 = (bf16[512,1536]{1,0:T(8,128)(2,1)S(1)}, bf16[512,1536]{1,0:T(8,128)(2,1)}, u32[]{:S(2)}) copy-start(bf16[512,1536]{1,0:T(8,128)(2,1)} %wqkv.1) | copy-start | bytes 4718596
  10.7 42.8 %copy-start.4 = (bf16[512,512]{1,0:T(8,128)(2,1)S(1)}, bf16[512,512]{1,0:T(8,128)(2,1)}, u32[]{:S(2)}) copy-start(bf16[512,512]{1,0:T(8,128)(2,1)} %wout.1) | copy-start | bytes 1572868
  10.7 42.7 %copy-start.5 = (bf16[256,512]{1,0:T(8,128)(2,1)S(1)}, bf16[256,512]{1,0:T(8,128)(2,1)}, u32[]{:S(2)}) copy-start(bf16[256,512]{1,0:T(8,128)(2,1)} %lift.1) | copy-start | bytes 786436
  10.7 42.7 %copy-start.6 = (bf16[512,256]{1,0:T(8,128)(2,1)S(1)}, bf16[512,256]{1,0:T(8,128)(2,1)}, u32[]{:S(2)}) copy-start(bf16[512,256]{1,0:T(8,128)(2,1)} %dec.1) | copy-start | bytes 786436
  10.7 42.7 %copy-start.7 = (f32[512]{0:T(512)S(1)}, f32[512]{0:T(512)}, u32[]{:S(2)}) copy-start(f32[512]{0:T(512)} %param.20) | copy-start | bytes 6148
  10.7 42.7 %copy-start.8 = (f32[512]{0:T(512)S(1)}, f32[512]{0:T(512)}, u32[]{:S(2)}) copy-start(f32[512]{0:T(512)} %param.23) | copy-start | bytes 6148

commit v3 on v2

--- a/solution.py
+++ b/solution.py
@@ -43,24 +43,17 @@
     return jnp.concatenate(parts, axis=1)
 
 
-def mix_kernel(
-    nbr_h, own_h, x_h, w1_h, w2_h, before, after, mixed, send, unpool,
-    nbr, own, x, w1, w2, sems, pick, gath, hot, share, *sums,
+def prepare_kernel(
+    nbr_h, own_h, x_h, w1_h, w2_h, x, w1, w2, pick, hot, unpool, share, nbr, own, sems
 ):
-    small = [
-        pltpu.make_async_copy(src, dst, sems.at[S_DEV + i])
-        for i, (src, dst) in enumerate(((nbr_h, nbr), (own_h, own), (w1_h, w1), (w2_h, w2)))
-    ]
-
-    def load(s):
-        return pltpu.make_async_copy(x_h.at[s], x.at[s], sems.at[s])
-
-    for copy in small:
+    pairs = ((nbr_h, nbr), (own_h, own), (w1_h, w1), (w2_h, w2)) + tuple(
+        (x_h.at[s], x.at[s]) for s in range(S_DEV)
+    )
+    copies = [pltpu.make_async_copy(src, dst, sems.at[i]) for i, (src, dst) in enumerate(pairs)]
+    for copy in copies:
         copy.start()
-    for s in range(S_DEV):
-        load(s).start()
-    small[0].wait()
-    small[1].wait()
+    copies[0].wait()
+    copies[1].wait()
     patch = lax.axis_index("patch")
     for j in range(8):
         for k in range(1, 5):
@@ -73,10 +66,36 @@
     onehot = (rows == slots).astype(f32)
     hot[...] = onehot.astype(bf16)
     share[...] = jnp.broadcast_to(1.0 / jnp.sum(onehot, axis=1, keepdims=True), (CC, TILE))
-
-    small[2].wait()
-    small[3].wait()
-
+    for copy in copies[2:]:
+        copy.wait()
+
+
+def prepare(nbr_t, own, x, w1, w2):
+    return pl.pallas_call(
+        prepare_kernel,
+        in_specs=[hbm] * 5,
+        out_specs=[vm] * 7,
+        out_shape=[
+            pltpu.VMEM((S_DEV, E_DEV, C), bf16),
+            pltpu.VMEM((5 * C, C), bf16),
+            pltpu.VMEM((C, C), bf16),
+            pltpu.VMEM((8, 4 * TILE, 2 * TILE), bf16),
+            pltpu.VMEM((CC, E_DEV), bf16),
+            jax.ShapeDtypeStruct((E_DEV, CC), bf16),
+            pltpu.VMEM((CC, TILE), f32),
+        ],
+        scratch_shapes=[
+            pltpu.VMEM((5, E_DEV), jnp.int32),
+            pltpu.VMEM((1, E_DEV), jnp.int32),
+            pltpu.SemaphoreType.DMA((S_DEV + 4,)),
+        ],
+        compiler_params=pltpu.CompilerParams(vmem_limit_bytes=16 * 2**20),
+        cost_estimate=pl.CostEstimate(flops=10**9, bytes_accessed=5 * 2**20, transcendentals=0),
+        name="prepare",
+    )(in_hbm(nbr_t), in_hbm(own), in_hbm(x), in_hbm(w1), in_hbm(w2))
+
+
+def mix_kernel(x, w1, w2, pick, hot, share, before, after, mixed, send, gath, *sums):
     def gather(s, base):
         for j in range(8):
             if j == 0:
@@ -91,8 +110,6 @@
                 gath[to, k * C : (k + 1) * C] = got[k * TILE : (k + 1) * TILE]
 
     def snapshots(b, _):
-        for i in range(SB):
-            load(b * SB + i).wait()
         for i in range(SB):
             gather(b * SB + i, i * E_DEV)
         centre = x[pl.ds(b * SB, SB)].reshape(SB * E_DEV, C)
@@ -118,34 +135,24 @@
 SB = 2
 
 
-def mix(nbr_t, own, x, before, after, w1, w2):
+def mix(x, w1, w2, pick, hot, share, before, after):
     return pl.pallas_call(
         mix_kernel,
-        in_specs=[hbm] * 5 + [vm] * 2,
-        out_specs=[vm] * 3,
+        in_specs=[vm] * 8,
+        out_specs=[vm] * 2,
         out_shape=[
             jax.ShapeDtypeStruct((S_DEV, E_DEV, C), bf16),
             jax.ShapeDtypeStruct((GROUPS, HC * S_DEV, C), bf16),
-            jax.ShapeDtypeStruct((E_DEV, CC), bf16),
         ],
         scratch_shapes=[
-            pltpu.VMEM((5, E_DEV), jnp.int32),
-            pltpu.VMEM((1, E_DEV), jnp.int32),
-            pltpu.VMEM((S_DEV, E_DEV, C), bf16),
-            pltpu.VMEM((5 * C, C), bf16),
-            pltpu.VMEM((C, C), bf16),
-            pltpu.SemaphoreType.DMA((S_DEV + 4,)),
-            pltpu.VMEM((8, 4 * TILE, 2 * TILE), bf16),
             pltpu.VMEM((SB * E_DEV, 4 * C), bf16),
-            pltpu.VMEM((CC, E_DEV), bf16),
-            pltpu.VMEM((CC, TILE), f32),
             pltpu.VMEM((CC * S_DEV, TILE), f32),
             pltpu.VMEM((CC * S_DEV, TILE), f32),
         ],
-        compiler_params=pltpu.CompilerParams(vmem_limit_bytes=32 * 2**20),
+        compiler_params=pltpu.CompilerParams(vmem_limit_bytes=26 * 2**20),
         cost_estimate=pl.CostEstimate(flops=12 * 10**9, bytes_accessed=2**20, transcendentals=2**21),
         name="mix",
-    )(in_hbm(nbr_t), in_hbm(own), in_hbm(x), in_hbm(w1), in_hbm(w2), before, after)
+    )(x, w1, w2, pick, hot, share, before, after)
 
 
 RB = 1024
@@ -293,13 +300,14 @@
     before = lax.ppermute(snapshots[:, E_DEV - HALO :], "patch", up)
     after = lax.ppermute(snapshots[:, :HALO], "patch", down)
     nbr_t = neighbours.T
-    mixed, send, hot = mix(
-        nbr_t, owners.reshape(1, E_DEV), snapshots, before, after, w_mix1, w_mix2
+    x, w1, w2, pick, hot, unpool, share = prepare(
+        nbr_t, owners.reshape(1, E_DEV), snapshots, w_mix1, w_mix2
     )
+    mixed, send = mix(x, w1, w2, pick, hot, share, before, after)
     weights = (w_lift, w_qkv, w_out, w_gate, w_up, w_down, w_dec)
     ga, gf = gain_attn.reshape(1, DC), gain_ffn.reshape(1, DC)
     back = exchange(layer(exchange(send), ga, gf, weights))
-    return spread(mixed, hot, back.reshape(ROWS, C))
+    return spread(mixed, unpool, back.reshape(ROWS, C))
 
 
 def solution(mesh):

time: 102 us -> 100 us (0.980)
  waiting for transfers between devices: 5.28 us -> 2.73 us
    ppermute x1, waiting for transfers between devices: 1.45 us -> 0.01 us  [per_device(): after = lax.ppermute(snapshots[:, :HALO], 'patch', down)]
    ppermute x1, waiting for transfers between devices: 3.82 us -> 2.73 us  [per_device(): before = lax.ppermute(snapshots[:, E_DEV - HALO:], 'patch', up)]
    pallas_call x1 -> x2, Pallas kernels: 19 us -> 19.4 us  [the longest x1 16.9 us: mix(): pl.pallas_call(mix_kernel, in_specs=[vm] * 8, out_specs=[vm] * 2, out_sha...]
  transfers between devices with their start and end apart: 2 -> 2, of which waited for: 2 -> 1; matrix products, arithmetic and copies ran while one was open for 0% -> 0% of each run, Pallas kernels for 0% -> 3%
where the time goes in v3:
time: 100 us
  Pallas kernels  48.5 us (48%)
  blocking collectives  42.9 us (43%)
  starting transfers between devices  4.33 us (4%)
  waiting for transfers between devices  2.73 us (3%)
  local copies, waits for them, and re-layouts  1.12 us (1%)
    all_to_all x2, blocking collectives, exchange(): return lax.all_to_all(x, 'tm', split_axis=0, concat_axis=0, tiled=True)  42.9 us
    pallas_call x1, Pallas kernels, layer(): pl.pallas_call(layer_kernel, in_specs=[vm] * 10, out_specs=vm, out_shape=...  26.4 us
    pallas_call x1, Pallas kernels, mix(): pl.pallas_call(mix_kernel, in_specs=[vm] * 8, out_specs=[vm] * 2, out_sha...  16.9 us
    ppermute x1, waiting for transfers between devices, per_device(): before = lax.ppermute(snapshots[:, E_DEV - HALO:], 'patch', up)  2.73 us
    pallas_call x1, Pallas kernels, spread(): pl.pallas_call(spread_kernel, in_specs=[vm, vm, vm], out_specs=hbm, out_s...  2.69 us
    pallas_call x1, Pallas kernels, prepare(): pl.pallas_call(prepare_kernel, in_specs=[hbm] * 5, out_specs=[vm] * 7, ou...  2.53 us
    ppermute x1, starting transfers between devices, per_device(): before = lax.ppermute(snapshots[:, E_DEV - HALO:], 'patch', up)  2.41 us
  transfers between devices with their start and end apart: 2, of which 1 were waited for; matrix products, arithmetic and copies ran while one was open for 0% of the time, Pallas kernels for 3%

profile of v3, /device:TPU:32, one launch (start us, length us, event | category | flops | bytes accessed | tf_op | source)
XLA Modules:
  0.0 100.0 jit_solution(16672223228469521101)
XLA Ops:
  0.0 1.1 %fusion = (bf16[8,64,256]{2,1,0:T(8,128)(2,1)S(1)}, bf16[8,64,256]{2,1,0:T(8,128)(2,1)S(1)}) fusion(bf16[8,1024,256]{2,1,0:T(8,128)(2,1)} %x_h.1), kind=kLoop, calls=%fused_computation | loop fusion | bytes 1048576 | tf_op jit(solution)/shard_map/slice | solution.py:301
  1.1 1.9 %collective-permute-start.1 = (bf16[8,64,256]{2,1,0:T(8,128)(2,1)S(1)}, bf16[8,64,256]{2,1,0:T(8,128)(2,1)S(1)}, u32[]{:S(2)}, u32[]{:S(2)}) collective-permute-start(bf16[8,64,256]{2,1,0:T(8,128)(2,1)S(1)} %get-tuple-element.23), channel_id=1, source_target_pairs={{1,0},{2,1},{3,2},{4,3},{5,4},{6,5},{7,6},{9,8},{10,9},{11,10},{12... | collective-permute-start | bytes 786440 | tf_op jit(solution)/shard_map/ppermute | solution.py:301
  3.0 2.4 %collective-permute-start = (bf16[8,64,256]{2,1,0:T(8,128)(2,1)S(1)}, bf16[8,64,256]{2,1,0:T(8,128)(2,1)S(1)}, u32[]{:S(2)}, u32[]{:S(2)}) collective-permute-start(bf16[8,64,256]{2,1,0:T(8,128)(2,1)S(1)} %get-tuple-element.24), channel_id=1, source_target_pairs={{0,1},{1,2},{2,3},{3,4},{4,5},{5,6},{6,7},{8,9},{9,10},{10,11},{11... | collective-permute-start | bytes 786440 | tf_op jit(solution)/shard_map/ppermute | solution.py:300
  5.4 2.5 %prepare.1 = (bf16[8,1024,256]{2,1,0:T(8,128)(2,1)S(1)}, bf16[1280,256]{1,0:T(8,128)(2,1)S(1)}, bf16[256,256]{1,0:T(8,128)(2,1)S(1)}, bf16[8,512,256]{2,1,0:T(8,...) custom-call(s32[5,1024]{1,0:T(8,128)} %bitcast.8, ...), custom_call_target="tpu_custom_call" | custom-call | flops 1000000000 | bytes 5242880 | tf_op jit(solution)/shard_map/prepare/pallas_call | solution.py:74
  8.0 0.0 collective-permute-done.1.after
  8.0 2.7 %collective-permute-done.before = bf16[8,64,256]{2,1,0:T(8,128)(2,1)S(1)} collective-permute-done((bf16[8,64,256]{2,1,0:T(8,128)(2,1)S(1)}, bf16[8,64,256]{2,1,0:T(8,128)(2,1)S(1)}, u32[]{:S(2)}, u32[]{:S(2)}) %collective-permute-start) | collective-permute-done | bytes 262176 | tf_op jit(solution)/shard_map/ppermute | solution.py:300
  10.7 0.0 copy-start.4
  10.7 0.0 copy-start.5
  10.7 0.0 copy-start.6
  10.7 0.0 copy-start.7
  10.8 0.0 copy-start.8
  10.8 16.9 %mix.1 = (bf16[8,1024,256]{2,1,0:T(8,128)(2,1)S(1)}, bf16[16,128,256]{2,1,0:T(8,128)(2,1)S(1)}) custom-call(bf16[8,1024,256]{2,1,0:T(8,128)(2,1)S(1)} %get-tuple-element.14.x, bf16[1280,256]{1,0:T(8,128)(2,1)S(1)} %get-tuple-element.15.w1, bf16[256,256]{1,0:T(8,128)(2,1)S(1)} %get-tuple-element.16.w2, bf16[8,512,256]{2,1,0:T(8,128)(2,1)S(1)} %get-tuple-element.17.pick, ...), custom_call_target="tpu_custom_call" | custom-call | flops 12000000000 | bytes 1048576 | tf_op jit(solution)/shard_map/mix/pallas_call | solution.py:139
  27.7 23.7 %all_to_all.10.x = bf16[16,128,256]{2,1,0:T(8,128)(2,1)S(1)} all-to-all(bf16[16,128,256]{2,1,0:T(8,128)(2,1)S(1)} %get-tuple-element.22), channel_id=1, replica_groups=mesh['tm'=16,'patch'=8] {'tm'}, dimensions={0} | all-to-all | bytes 2097152 | tf_op jit(solution)/shard_map/all_to_all | solution.py:290
  51.4 0.0 copy-done
  51.4 0.0 copy-done.2
  51.4 0.0 copy-done.3
  51.4 0.0 copy-done.4
  51.4 0.0 copy-done.5
  51.4 0.0 copy-done.6
  51.4 0.0 copy-done.7
  51.5 0.0 copy-done.8
  51.5 26.4 %layer.1 = bf16[16,128,256]{2,1,0:T(8,128)(2,1)S(1)} custom-call(bf16[16,128,256]{2,1,0:T(8,128)(2,1)S(1)} %all_to_all.10.x, f32[1,512]{1,0:T(1,128)S(1)} %bitcast.6, f32[1,512]{1,0:T(1,128)S(1)} %bitcast.7, bf16[256,512]{1,0:T(8,128)(2,1)S(1)} %copy-done.5, bf16[512,1536]{1,0:T(8,128)(2,1)S(1)} %copy-done.3, bf16[512,512]{1,0:T(8,128)(2,1)S(1)} %copy-done.4, ...), custom_call_target="tpu_custom_call" | custom-call | flops 24000000000 | bytes 1048576 | tf_op jit(solution)/shard_map/layer/pallas_call | solution.py:231
  77.9 19.2 %all_to_all.11 = bf16[16,128,256]{2,1,0:T(8,128)(2,1)S(1)} all-to-all(bf16[16,128,256]{2,1,0:T(8,128)(2,1)S(1)} %layer.1), channel_id=1, replica_groups=mesh['tm'=16,'patch'=8] {'tm'}, dimensions={0} | all-to-all | bytes 2097152 | tf_op jit(solution)/shard_map/all_to_all | solution.py:290
  97.1 2.7 %spread.1 = bf16[8,1024,256]{2,1,0:T(8,128)(2,1)} custom-call(bf16[8,1024,256]{2,1,0:T(8,128)(2,1)S(1)} %get-tuple-element.20.mixed, bf16[1024,256]{1,0:T(8,128)(2,1)S(1)} %get-tuple-element.21.hot, bf16[2048,256]{1,0:T(8,128)(2,1)S(1)} %bitcast.5), custom_call_target="tpu_custom_call" | custom-call | flops 1000000000 | bytes 8388608 | tf_op jit(solution)/shard_map/spread/pallas_call | solution.py:268
  (5 shorter events, 0.0 us)
Async XLA Ops:
  1.1 6.9 %collective-permute-start.1 = (bf16[8,64,256]{2,1,0:T(8,128)(2,1)S(1)}, bf16[8,64,256]{2,1,0:T(8,128)(2,1)S(1)}, u32[]{:S(2)}, u32[]{:S(2)}) collective-permute-start(bf16[8,64,256]{2,1,0:T(8,128)(2,1)S(1)} %get-tuple-element.23), channel_id=1, source_target_pairs={{1,0},{2,1},{3,2},{4,3},{5,4},{6,5},{7,6},{9,8},{10,9},{11,10},{12... | collective-permute-start | bytes 786440 | tf_op jit(solution)/shard_map/ppermute | solution.py:301
  3.0 7.7 %collective-permute-start = (bf16[8,64,256]{2,1,0:T(8,128)(2,1)S(1)}, bf16[8,64,256]{2,1,0:T(8,128)(2,1)S(1)}, u32[]{:S(2)}, u32[]{:S(2)}) collective-permute-start(bf16[8,64,256]{2,1,0:T(8,128)(2,1)S(1)} %get-tuple-element.24), channel_id=1, source_target_pairs={{0,1},{1,2},{2,3},{3,4},{4,5},{5,6},{6,7},{8,9},{9,10},{10,11},{11... | collective-permute-start | bytes 786440 | tf_op jit(solution)/shard_map/ppermute | solution.py:300
  10.7 40.7 %copy-start = (bf16[512,2048]{1,0:T(8,128)(2,1)S(1)}, bf16[512,2048]{1,0:T(8,128)(2,1)}, u32[]{:S(2)}) copy-start(bf16[512,2048]{1,0:T(8,128)(2,1)} %gate.1) | copy-start | bytes 6291460
  10.7 40.7 %copy-start.1 = (bf16[512,2048]{1,0:T(8,128)(2,1)S(1)}, bf16[512,2048]{1,0:T(8,128)(2,1)}, u32[]{:S(2)}) copy-start(bf16[512,2048]{1,0:T(8,128)(2,1)} %up.1) | copy-start | bytes 6291460
  10.7 40.7 %copy-start.2 = (bf16[2048,512]{1,0:T(8,128)(2,1)S(1)}, bf16[2048,512]{1,0:T(8,128)(2,1)}, u32[]{:S(2)}) copy-start(bf16[2048,512]{1,0:T(8,128)(2,1)} %down.1) | copy-start | bytes 6291460
  10.7 40.7 %copy-start.3 = (bf16[512,1536]{1,0:T(8,128)(2,1)S(1)}, bf16[512,1536]{1,0:T(8,128)(2,1)}, u32[]{:S(2)}) copy-start(bf16[512,1536]{1,0:T(8,128)(2,1)} %wqkv.1) | copy-start | bytes 4718596
  10.7 40.7 %copy-start.4 = (bf16[512,512]{1,0:T(8,128)(2,1)S(1)}, bf16[512,512]{1,0:T(8,128)(2,1)}, u32[]{:S(2)}) copy-start(bf16[512,512]{1,0:T(8,128)(2,1)} %wout.1) | copy-start | bytes 1572868
  10.7 40.7 %copy-start.5 = (bf16[256,512]{1,0:T(8,128)(2,1)S(1)}, bf16[256,512]{1,0:T(8,128)(2,1)}, u32[]{:S(2)}) copy-start(bf16[256,512]{1,0:T(8,128)(2,1)} %lift.1) | copy-start | bytes 786436
  10.7 40.7 %copy-start.6 = (bf16[512,256]{1,0:T(8,128)(2,1)S(1)}, bf16[512,256]{1,0:T(8,128)(2,1)}, u32[]{:S(2)}) copy-start(bf16[512,256]{1,0:T(8,128)(2,1)} %dec.1) | copy-start | bytes 786436
  10.7 40.7 %copy-start.7 = (f32[512]{0:T(512)S(1)}, f32[512]{0:T(512)}, u32[]{:S(2)}) copy-start(f32[512]{0:T(512)} %param.20) | copy-start | bytes 6148
  10.8 40.7 %copy-start.8 = (f32[512]{0:T(512)S(1)}, f32[512]{0:T(512)}, u32[]{:S(2)}) copy-start(f32[512]{0:T(512)} %param.23) | copy-start | bytes 6148

commit v4 on v3

--- a/solution.py
+++ b/solution.py
@@ -31,8 +31,11 @@
 
 
 def gelu(x):
-    inner = 0.7978845608028654 * (x + 0.044715 * (x * x * x))
-    return 0.5 * x * (1.0 + jnp.tanh(inner))
+    scaled = (0.7978845608028654 * x).astype(bf16)
+    short = x.astype(bf16)
+    inner = scaled + scaled * (short * short * jnp.bfloat16(0.044715))
+    half = short * jnp.bfloat16(0.5)
+    return half + half * jnp.tanh(inner)
 
 
 def pick_rows(ids_row, width=2 * TILE):
@@ -114,7 +117,7 @@
             gather(b * SB + i, i * E_DEV)
         centre = x[pl.ds(b * SB, SB)].reshape(SB * E_DEV, C)
         pre = dot(centre, w1[0:C, :]) + dot(gath[...], w1[C:, :])
-        act = gelu(pre).astype(bf16)
+        act = gelu(pre)
         both = (centre.astype(f32) + dot(act, w2[...])).astype(bf16)
         mixed[pl.ds(b * SB, SB)] = both.reshape(SB, E_DEV, C)
         for i in range(SB):
@@ -220,7 +223,7 @@
         flat[pl.ds(r0, RB), :] = dot(two, dec[...])
         return 0
 
-    lax.fori_loop(0, ROWS // RB, block, 0)
+    lax.fori_loop(0, ROWS // RB, block, 0, unroll=True)
     for g in range(GROUPS):
         y[g] = jnp.concatenate(
             [flat[c * 128 + g * S_DEV : c * 128 + (g + 1) * S_DEV, :] for c in range(HC)], axis=0

time: 100 us -> 98.6 us (0.986)
  Pallas kernels: 48.5 us -> 47 us
where the time goes in v4:
time: 98.6 us; the launch traced here: 98.4 us
  Pallas kernels  47 us (48%)
  blocking collectives  42.9 us (44%)
  starting transfers between devices  4.33 us (4%)
  waiting for transfers between devices  2.73 us (3%)
  local copies, waits for them, and re-layouts  1.12 us (1%)
    all_to_all x2, blocking collectives, exchange(): return lax.all_to_all(x, 'tm', split_axis=0, concat_axis=0, tiled=True)  42.9 us
    pallas_call x1, Pallas kernels, layer(): pl.pallas_call(layer_kernel, in_specs=[vm] * 10, out_specs=vm, out_shape=...  25.7 us
    pallas_call x1, Pallas kernels, mix(): pl.pallas_call(mix_kernel, in_specs=[vm] * 8, out_specs=[vm] * 2, out_sha...  16.1 us
    ppermute x1, waiting for transfers between devices, per_device(): before = lax.ppermute(snapshots[:, E_DEV - HALO:], 'patch', up)  2.73 us
    pallas_call x1, Pallas kernels, spread(): pl.pallas_call(spread_kernel, in_specs=[vm, vm, vm], out_specs=hbm, out_s...  2.7 us
    pallas_call x1, Pallas kernels, prepare(): pl.pallas_call(prepare_kernel, in_specs=[hbm] * 5, out_specs=[vm] * 7, ou...  2.53 us
    ppermute x1, starting transfers between devices, per_device(): before = lax.ppermute(snapshots[:, E_DEV - HALO:], 'patch', up)  2.41 us
  transfers between devices with their start and end apart: 2, of which 1 were waited for; matrix products, arithmetic and copies ran while one was open for 0% of the time, Pallas kernels for 3%

profile of v4, /device:TPU:32, one launch (start us, length us, event | category | flops | bytes accessed | tf_op | source)
XLA Modules:
  0.0 98.4 jit_solution(2951637706669693757)
XLA Ops:
  0.0 1.1 %fusion = (bf16[8,64,256]{2,1,0:T(8,128)(2,1)S(1)}, bf16[8,64,256]{2,1,0:T(8,128)(2,1)S(1)}) fusion(bf16[8,1024,256]{2,1,0:T(8,128)(2,1)} %x_h.1), kind=kLoop, calls=%fused_computation | loop fusion | bytes 1048576 | tf_op jit(solution)/shard_map/slice | solution.py:304
  1.1 1.9 %collective-permute-start.1 = (bf16[8,64,256]{2,1,0:T(8,128)(2,1)S(1)}, bf16[8,64,256]{2,1,0:T(8,128)(2,1)S(1)}, u32[]{:S(2)}, u32[]{:S(2)}) collective-permute-start(bf16[8,64,256]{2,1,0:T(8,128)(2,1)S(1)} %get-tuple-element.23), channel_id=1, source_target_pairs={{1,0},{2,1},{3,2},{4,3},{5,4},{6,5},{7,6},{9,8},{10,9},{11,10},{12... | collective-permute-start | bytes 786440 | tf_op jit(solution)/shard_map/ppermute | solution.py:304
  3.0 2.4 %collective-permute-start = (bf16[8,64,256]{2,1,0:T(8,128)(2,1)S(1)}, bf16[8,64,256]{2,1,0:T(8,128)(2,1)S(1)}, u32[]{:S(2)}, u32[]{:S(2)}) collective-permute-start(bf16[8,64,256]{2,1,0:T(8,128)(2,1)S(1)} %get-tuple-element.24), channel_id=1, source_target_pairs={{0,1},{1,2},{2,3},{3,4},{4,5},{5,6},{6,7},{8,9},{9,10},{10,11},{11... | collective-permute-start | bytes 786440 | tf_op jit(solution)/shard_map/ppermute | solution.py:303
  5.4 2.5 %prepare.1 = (bf16[8,1024,256]{2,1,0:T(8,128)(2,1)S(1)}, bf16[1280,256]{1,0:T(8,128)(2,1)S(1)}, bf16[256,256]{1,0:T(8,128)(2,1)S(1)}, bf16[8,512,256]{2,1,0:T(8,...) custom-call(s32[5,1024]{1,0:T(8,128)} %bitcast.8, ...), custom_call_target="tpu_custom_call" | custom-call | flops 1000000000 | bytes 5242880 | tf_op jit(solution)/shard_map/prepare/pallas_call | solution.py:77
  8.0 0.0 collective-permute-done.1.after
  8.0 2.7 %collective-permute-done.before = bf16[8,64,256]{2,1,0:T(8,128)(2,1)S(1)} collective-permute-done((bf16[8,64,256]{2,1,0:T(8,128)(2,1)S(1)}, bf16[8,64,256]{2,1,0:T(8,128)(2,1)S(1)}, u32[]{:S(2)}, u32[]{:S(2)}) %collective-permute-start) | collective-permute-done | bytes 262176 | tf_op jit(solution)/shard_map/ppermute | solution.py:303
  10.7 0.0 copy-start.4
  10.7 0.0 copy-start.5
  10.7 0.0 copy-start.6
  10.7 0.0 copy-start.7
  10.8 0.0 copy-start.8
  10.8 16.1 %mix.1 = (bf16[8,1024,256]{2,1,0:T(8,128)(2,1)S(1)}, bf16[16,128,256]{2,1,0:T(8,128)(2,1)S(1)}) custom-call(bf16[8,1024,256]{2,1,0:T(8,128)(2,1)S(1)} %get-tuple-element.14.x, bf16[1280,256]{1,0:T(8,128)(2,1)S(1)} %get-tuple-element.15.w1, bf16[256,256]{1,0:T(8,128)(2,1)S(1)} %get-tuple-element.16.w2, bf16[8,512,256]{2,1,0:T(8,128)(2,1)S(1)} %get-tuple-element.17.pick, ...), custom_call_target="tpu_custom_call" | custom-call | flops 12000000000 | bytes 1048576 | tf_op jit(solution)/shard_map/mix/pallas_call | solution.py:142
  26.8 23.7 %all_to_all.10.x = bf16[16,128,256]{2,1,0:T(8,128)(2,1)S(1)} all-to-all(bf16[16,128,256]{2,1,0:T(8,128)(2,1)S(1)} %get-tuple-element.22), channel_id=1, replica_groups=mesh['tm'=16,'patch'=8] {'tm'}, dimensions={0} | all-to-all | bytes 2097152 | tf_op jit(solution)/shard_map/all_to_all | solution.py:293
  50.5 0.0 copy-done
  50.5 0.0 copy-done.1
  50.5 0.0 copy-done.2
  50.5 0.0 copy-done.3
  50.5 0.0 copy-done.4
  50.6 0.0 copy-done.5
  50.6 0.0 copy-done.6
  50.6 0.0 copy-done.7
  50.6 25.7 %layer.1 = bf16[16,128,256]{2,1,0:T(8,128)(2,1)S(1)} custom-call(bf16[16,128,256]{2,1,0:T(8,128)(2,1)S(1)} %all_to_all.10.x, f32[1,512]{1,0:T(1,128)S(1)} %bitcast.6, f32[1,512]{1,0:T(1,128)S(1)} %bitcast.7, bf16[256,512]{1,0:T(8,128)(2,1)S(1)} %copy-done.5, bf16[512,1536]{1,0:T(8,128)(2,1)S(1)} %copy-done.3, bf16[512,512]{1,0:T(8,128)(2,1)S(1)} %copy-done.4, ...), custom_call_target="tpu_custom_call" | custom-call | flops 24000000000 | bytes 1048576 | tf_op jit(solution)/shard_map/layer/pallas_call | solution.py:234
  76.3 19.2 %all_to_all.11 = bf16[16,128,256]{2,1,0:T(8,128)(2,1)S(1)} all-to-all(bf16[16,128,256]{2,1,0:T(8,128)(2,1)S(1)} %layer.1), channel_id=1, replica_groups=mesh['tm'=16,'patch'=8] {'tm'}, dimensions={0} | all-to-all | bytes 2097152 | tf_op jit(solution)/shard_map/all_to_all | solution.py:293
  95.5 2.7 %spread.1 = bf16[8,1024,256]{2,1,0:T(8,128)(2,1)} custom-call(bf16[8,1024,256]{2,1,0:T(8,128)(2,1)S(1)} %get-tuple-element.20.mixed, bf16[1024,256]{1,0:T(8,128)(2,1)S(1)} %get-tuple-element.21.hot, bf16[2048,256]{1,0:T(8,128)(2,1)S(1)} %bitcast.5), custom_call_target="tpu_custom_call" | custom-call | flops 1000000000 | bytes 8388608 | tf_op jit(solution)/shard_map/spread/pallas_call | solution.py:271
  (5 shorter events, 0.0 us)
Async XLA Ops:
  1.1 6.9 %collective-permute-start.1 = (bf16[8,64,256]{2,1,0:T(8,128)(2,1)S(1)}, bf16[8,64,256]{2,1,0:T(8,128)(2,1)S(1)}, u32[]{:S(2)}, u32[]{:S(2)}) collective-permute-start(bf16[8,64,256]{2,1,0:T(8,128)(2,1)S(1)} %get-tuple-element.23), channel_id=1, source_target_pairs={{1,0},{2,1},{3,2},{4,3},{5,4},{6,5},{7,6},{9,8},{10,9},{11,10},{12... | collective-permute-start | bytes 786440 | tf_op jit(solution)/shard_map/ppermute | solution.py:304
  3.0 7.7 %collective-permute-start = (bf16[8,64,256]{2,1,0:T(8,128)(2,1)S(1)}, bf16[8,64,256]{2,1,0:T(8,128)(2,1)S(1)}, u32[]{:S(2)}, u32[]{:S(2)}) collective-permute-start(bf16[8,64,256]{2,1,0:T(8,128)(2,1)S(1)} %get-tuple-element.24), channel_id=1, source_target_pairs={{0,1},{1,2},{2,3},{3,4},{4,5},{5,6},{6,7},{8,9},{9,10},{10,11},{11... | collective-permute-start | bytes 786440 | tf_op jit(solution)/shard_map/ppermute | solution.py:303
  10.7 39.8 %copy-start = (bf16[512,2048]{1,0:T(8,128)(2,1)S(1)}, bf16[512,2048]{1,0:T(8,128)(2,1)}, u32[]{:S(2)}) copy-start(bf16[512,2048]{1,0:T(8,128)(2,1)} %gate.1) | copy-start | bytes 6291460
  10.7 39.8 %copy-start.1 = (bf16[512,2048]{1,0:T(8,128)(2,1)S(1)}, bf16[512,2048]{1,0:T(8,128)(2,1)}, u32[]{:S(2)}) copy-start(bf16[512,2048]{1,0:T(8,128)(2,1)} %up.1) | copy-start | bytes 6291460
  10.7 39.8 %copy-start.2 = (bf16[2048,512]{1,0:T(8,128)(2,1)S(1)}, bf16[2048,512]{1,0:T(8,128)(2,1)}, u32[]{:S(2)}) copy-start(bf16[2048,512]{1,0:T(8,128)(2,1)} %down.1) | copy-start | bytes 6291460
  10.7 39.8 %copy-start.3 = (bf16[512,1536]{1,0:T(8,128)(2,1)S(1)}, bf16[512,1536]{1,0:T(8,128)(2,1)}, u32[]{:S(2)}) copy-start(bf16[512,1536]{1,0:T(8,128)(2,1)} %wqkv.1) | copy-start | bytes 4718596
  10.7 39.8 %copy-start.4 = (bf16[512,512]{1,0:T(8,128)(2,1)S(1)}, bf16[512,512]{1,0:T(8,128)(2,1)}, u32[]{:S(2)}) copy-start(bf16[512,512]{1,0:T(8,128)(2,1)} %wout.1) | copy-start | bytes 1572868
  10.7 39.8 %copy-start.5 = (bf16[256,512]{1,0:T(8,128)(2,1)S(1)}, bf16[256,512]{1,0:T(8,128)(2,1)}, u32[]{:S(2)}) copy-start(bf16[256,512]{1,0:T(8,128)(2,1)} %lift.1) | copy-start | bytes 786436
  10.7 39.8 %copy-start.6 = (bf16[512,256]{1,0:T(8,128)(2,1)S(1)}, bf16[512,256]{1,0:T(8,128)(2,1)}, u32[]{:S(2)}) copy-start(bf16[512,256]{1,0:T(8,128)(2,1)} %dec.1) | copy-start | bytes 786436
  10.7 39.8 %copy-start.7 = (f32[512]{0:T(512)S(1)}, f32[512]{0:T(512)}, u32[]{:S(2)}) copy-start(f32[512]{0:T(512)} %param.20) | copy-start | bytes 6148
  10.8 39.8 %copy-start.8 = (f32[512]{0:T(512)S(1)}, f32[512]{0:T(512)}, u32[]{:S(2)}) copy-start(f32[512]{0:T(512)} %param.23) | copy-start | bytes 6148
